TPU v7x, 256 devices: a whole 4x4x8 slice. The times are simulated.
256 devices in a mesh: row: 32 (over x, z_hi, core), col: 8 (over y, z_lo).
Axes of the slice: x: 4, y: 4, z: 8 (z_hi: 4, z_lo: 2; z = z_hi * 2 + z_lo), core: 2. Of those that a mesh axis runs over, the one named last changes fastest.
Arguments:
- x_train: bfloat16 [64, 32768], P(None, 'col'), may hold values from -8 to 8
- targets: float32 [32768], P('col'), may hold values from -6 to 6
- noise_draws: float32 [32768, 256], P('col', 'row'), may hold values from -3 to 3
- alpha_init: float32 [32768, 256], P('col', 'row'), may hold values from -6 to 6
- velocity_init: float32 [32768, 256], P('col', 'row'), may hold values from -3 to 3
- frequencies: bfloat16 [64, 4096], P(None, 'col'), may hold values from -5 to 5
- phases: float32 [4096], P('col'), may hold values from -3.140625 to 3.140625
- path_weights: bfloat16 [4096, 256], P('col'), may hold values from -6 to 6
- x_window: bfloat16 [64, 65536], P(None, 'row'), may hold values from -6 to 6
- batch_index: int32 [3, 16384], replicated, may hold values from 0 to 32767, as said below
Outputs:
- alpha_out: float32 [32768, 256], P('col', 'row')
- velocity_out: float32 [32768, 256], P('col', 'row')
- prior_window: float32 [256, 65536], P('col', 'row')
Inputs may be any that keep to these rules, and one draw needn't show every extreme that they name: `batch_index`: row b of every step names a training point of group g = (b // 64) % 8, that is a number from g * 4096 to (g + 1) * 4096 - 1; points may repeat.
All inputs are finite; a program needn't handle non-finite values.
Results may differ from a plain program's by a relative error of at most 0.0039.
Values may be sent and summed in bfloat16 or wider, within the bound.
No kernel may reach another device: no remote copies, remote signals or barrier semaphores. Data moves between devices by JAX's collectives and lax.ppermute only.
A program may use at most 64 MiB of HBM per device.

v0:
```python
import jax
import jax.numpy as jnp
from jax import lax
from jax.sharding import PartitionSpec as P

FEAT = 4096
STEPS = 3


SQRT_THREE = 1.7320508075688772
LENGTH = 1.15
NOISE_VAR = 0.25
MOMENTUM = 0.9
STEP_SIZE = 0.5
HIGH = lax.Precision.HIGHEST


def features(points, frequencies, phases):
    phase_arg = lax.dot_general(
        frequencies, points, (((0,), (0,)), ((), ())), preferred_element_type=jnp.float32
    )
    factor = (2.0 / FEAT) ** 0.5
    return (factor * jnp.cos(phase_arg + phases[:, None])).astype(jnp.bfloat16)


def kernel_rows(points, x_train, train_norm):
    inner_prod = lax.dot_general(
        points, x_train, (((0,), (0,)), ((), ())), preferred_element_type=jnp.float32
    )
    point_norm = jnp.sum(jnp.square(points.astype(jnp.float32)), axis=0)
    dist_sq = jnp.maximum(point_norm[:, None] + train_norm[None, :] - 2.0 * inner_prod, 0.0)
    scaled = SQRT_THREE / LENGTH * jnp.sqrt(dist_sq)
    return ((1.0 + scaled) * jnp.exp(-scaled)).astype(jnp.bfloat16)


def shards(
    x_train,
    targets,
    noise_draws,
    alpha_init,
    velocity_init,
    frequencies,
    phases,
    path_weights,
    x_window,
    batch_index,
):
    row_count = lax.axis_size("row")
    col_count = lax.axis_size("col")
    row_id = lax.axis_index("row")
    col_id = lax.axis_index("col")
    train_cols = x_train.shape[1]
    batch_rows = batch_index.shape[1] // row_count
    own_rows = batch_rows // col_count
    col_start = col_id * train_cols
    my_index = lax.dynamic_slice_in_dim(batch_index, row_id * batch_rows, batch_rows, 1)
    flat_index = my_index.reshape(-1)
    column_ids = lax.broadcasted_iota(jnp.int32, (train_cols, 1), 0)
    selector = (column_ids == (flat_index - col_start)[None, :]).astype(jnp.bfloat16)
    picked = jnp.dot(x_train, selector, preferred_element_type=jnp.float32)
    batch_points = lax.psum(picked.astype(jnp.bfloat16), "col")
    phi_window = features(x_window, frequencies, phases)
    prior_window = lax.psum_scatter(
        lax.dot_general(
            path_weights, phi_window, (((0,), (0,)), ((), ())), preferred_element_type=jnp.float32
        ),
        "col",
        scatter_dimension=0,
        tiled=True,
    )
    train_norm = jnp.sum(jnp.square(x_train.astype(jnp.float32)), axis=0)
    block_rows = min(256, batch_rows)
    block_count = batch_rows // block_rows
    dual_state, velocity, noise_rows = (alpha_init, velocity_init, noise_draws)
    slot_ids = lax.broadcasted_iota(jnp.int32, (1, train_cols), 1)
    for step_id in range(STEPS):
        points_now = batch_points[:, step_id * batch_rows : (step_id + 1) * batch_rows]
        point_blocks = points_now.reshape(x_train.shape[0], block_count, block_rows).transpose(
            1, 0, 2
        )
        kernel_tile = lax.map(
            lambda block_points: kernel_rows(block_points, x_train, train_norm), point_blocks
        )
        kernel_tile = kernel_tile.reshape(batch_rows, train_cols)
        phi_batch = features(points_now, frequencies, phases)
        prior_rows = lax.dot_general(
            phi_batch, path_weights, (((0,), (0,)), ((), ())), preferred_element_type=jnp.float32
        )
        coeffs = dual_state.astype(jnp.bfloat16)
        coeffs = lax.all_gather(coeffs, "row", axis=1, tiled=True)
        coupled = jnp.dot(kernel_tile, coeffs, preferred_element_type=jnp.float32)
        partial_sum = coupled + prior_rows
        summed = lax.psum(partial_sum, "col")
        owned_rows = lax.dynamic_slice_in_dim(summed, col_id * own_rows, own_rows, 0)
        arrived = lax.all_to_all(owned_rows, "row", split_axis=1, concat_axis=0, tiled=True)
        step_index = batch_index[step_id].reshape(row_count, col_count, own_rows)
        owner_slot = lax.dynamic_slice_in_dim(step_index, col_id, 1, 1).reshape(-1) - col_start
        owner_slot = jnp.clip(owner_slot, 0, train_cols - 1)
        point_terms = NOISE_VAR * dual_state - targets[:, None] + noise_rows
        owner_map = (owner_slot[:, None] == slot_ids).astype(jnp.float32)
        row_terms = arrived + jnp.dot(owner_map, point_terms, precision=HIGH)
        gradient = lax.dot_general(owner_map, row_terms, (((0,), (0,)), ((), ())), precision=HIGH)
        velocity = MOMENTUM * velocity - STEP_SIZE * gradient
        dual_state = dual_state + velocity
    return (dual_state, velocity, prior_window)


def solution(mesh):
    placed = (
        P(None, "col"),
        P("col"),
        P("col", "row"),
        P("col", "row"),
        P("col", "row"),
        P(None, "col"),
        P("col"),
        P("col", None),
        P(None, "row"),
        P(),
    )
    return jax.shard_map(
        shards,
        mesh=mesh,
        in_specs=placed,
        out_specs=(P("col", "row"), P("col", "row"), P("col", "row")),
        check_vma=False,
    )
```

profile of v0, /device:TPU:1, one launch (start us, length us, event | category | flops | bytes accessed | tf_op | source)
XLA Modules:
  0.0 627.6 jit_solution(13569463593673693496)
XLA Ops:
  8.1 0.7 dynamic-slice_subtract_fusion
  8.8 6.0 fusion.48
  14.9 0.6 convert_element_type.58
  15.6 0.2 all-reduce.7.cloned.1.call-start
  15.8 0.1 multiply_reduce_fusion.3
  16.0 76.1 %all-reduce.5.cloned.1.call-done = bf16[64,1536]{1,0:T(8,128)(2,1)} async-done(((bf16[64,1536]{1,0:T(8,128)(2,1)}), bf16[64,1536]{1,0:T(8,128)(2,1)}) %all-reduce.5.cloned.1.call-update) | async-done | bytes 196624 | tf_op jit(solution)/shard_map/psum | solution.py:61
  92.1 0.9 fusion.103
  93.0 2.4 broadcast.121.clone
  95.5 8.1 %while.30 = (s32[]{:T(128)}, bf16[2,256,4096]{2,1,0:T(8,128)(2,1)}, bf16[2,64,256]{2,1,0:T(8,128)(2,1)S(1)}, f32[4096]{0:T(1024)S(1)}, bf16[64,4096]{1,0:T(8,128)(2,1)S(1)}, /*index=5*/s32[]{:T(128)}) while((s32[]{:T(128)}, bf16[2,256,4096]{2,1,0:T(8,128)(2,1)}, bf16[2,64,256]{2,1,0:T(8,128)(2,1)S(1)}, f32[4096]{0:T(1024)S(1)}, ...), condition=%wide.region_4.0_spmd, body=%wide.region_2.4_spmd.sunk | while | flops 143703808 | bytes 2706513 | solution.py:81
  95.5 4.1 fusion.141
  99.6 4.0 fusion.141
  103.6 4.2 fusion.105
  107.9 4.7 fusion.64
  112.6 79.9 %all-reduce.7.cloned.1.call-done = f32[512,256]{1,0:T(8,128)} async-done(((f32[512,256]{1,0:T(8,128)}), f32[512,256]{1,0:T(8,128)}) %all-reduce.7.cloned.1.call-update) | async-done | bytes 524304 | tf_op jit(solution)/shard_map/psum | solution.py:93
  192.5 0.8 constant_dynamic-slice_fusion.2
  193.5 0.8 reshape.125
  194.3 14.0 %all-to-all-start = ((f32[32,1,512]{2,1,0:T(1,128)}), f32[32,1,512]{2,1,0:T(1,128)S(1)}, u32[]{:S(2)}, u32[]{:S(2)}) async-start(f32[32,1,512]{2,1,0:T(1,128)} %reshape.125), calls=%async_computation | async-start | bytes 131072 | tf_op jit(solution)/shard_map/all_to_all | solution.py:95
  208.3 0.3 all-gather.6.cloned.1.call-start
  208.6 0.5 slice_reduce_fusion
  209.3 8.7 %all-to-all-done = f32[32,1,512]{2,1,0:T(1,128)S(1)} async-done(((f32[32,1,512]{2,1,0:T(1,128)}), f32[32,1,512]{2,1,0:T(1,128)S(1)}, u32[]{:S(2)}, u32[]{:S(2)}) %all-to-all-start) | async-done | bytes 65568 | tf_op jit(solution)/shard_map/all_to_all | solution.py:95
  218.0 0.5 broadcast.185
  218.5 0.7 reduce.24
  219.4 0.1 all_to_all.45
  219.5 15.3 %fusion.49 = f32[2048,8]{0,1:T(8,128)S(1)} fusion(f32[2048,8]{0,1:T(8,128)S(1)} %all_to_all.45, s32[2048]{0:T(1024)S(1)} %min.24, f32[4096,8]{0,1:T(8,128)S(1)} %copy-done.7, f32[4096,8]{0,1:T(8,128)S(1)} %copy-done.4, f32[4096]{0:T(1024)S(1)} %copy-done.9), kind=kOutput, calls=%fused_computation.64 | convolution fusion | flops 813809664 | bytes 417792 | tf_op jit(solution)/shard_map/dot_general | solution.py:101
  234.9 11.2 %fusion.102 = (bf16[4096,8]{0,1:T(8,128)(2,1)}, f32[4096,8]{0,1:T(8,128)S(1)}, f32[4096,8]{0,1:T(8,128)S(1)}) fusion(f32[4096,8]{0,1:T(8,128)S(1)} %copy-done.4, f32[2048,8]{0,1:T(8,128)S(1)} %fusion.49, s32[2048]{0:T(1024)S(1)} %min.24, f32[4096,8]{0,1:T(8,128)S(1)} %copy-done.6), kind=kOutput, calls=%fused_computation.131 | convolution fusion | flops 813858816 | bytes 663552 | tf_op jit(solution)/shard_map/dot_general | solution.py:102
  246.1 0.2 all-reduce.9.cloned.1.call-start
  246.3 2.4 broadcast.121.clone.1
  248.8 8.1 %while.31 = (s32[]{:T(128)}, bf16[2,256,4096]{2,1,0:T(8,128)(2,1)}, bf16[2,64,256]{2,1,0:T(8,128)(2,1)S(1)}, f32[4096]{0:T(1024)S(1)}, bf16[64,4096]{1,0:T(8,128)(2,1)S(1)}, /*index=5*/s32[]{:T(128)}) while((s32[]{:T(128)}, bf16[2,256,4096]{2,1,0:T(8,128)(2,1)}, bf16[2,64,256]{2,1,0:T(8,128)(2,1)S(1)}, f32[4096]{0:T(1024)S(1)}, ...), condition=%wide.region_8.9_spmd, body=%wide.region_6.8_spmd.sunk | while | flops 143703808 | bytes 2706513 | solution.py:81
  248.8 4.1 fusion.144
  252.9 4.0 fusion.144
  256.9 37.7 %all-gather.6.cloned.1.call-done = bf16[4096,256]{0,1:T(8,128)(2,1)} async-done(((bf16[4096,8]{0,1:T(8,128)(2,1)}), bf16[4096,256]{0,1:T(8,128)(2,1)}) %all-gather.6.cloned.1.call-update) | async-done | bytes 2097168 | tf_op jit(solution)/shard_map/all_gather | solution.py:90
  294.6 4.1 fusion.106
  298.8 4.7 fusion.65
  303.5 72.4 %all-reduce.9.cloned.1.call-done = f32[512,256]{1,0:T(8,128)} async-done(((f32[512,256]{1,0:T(8,128)}), f32[512,256]{1,0:T(8,128)}) %all-reduce.9.cloned.1.call-update) | async-done | bytes 524304 | tf_op jit(solution)/shard_map/psum | solution.py:93
  375.9 0.8 constant_dynamic-slice_fusion.1
  376.9 0.8 reshape.127
  377.6 14.0 %all-to-all-start.1 = ((f32[32,1,512]{2,1,0:T(1,128)}), f32[32,1,512]{2,1,0:T(1,128)S(1)}, u32[]{:S(2)}, u32[]{:S(2)}) async-start(f32[32,1,512]{2,1,0:T(1,128)} %reshape.127), calls=%async_computation.1 | async-start | bytes 131072 | tf_op jit(solution)/shard_map/all_to_all | solution.py:95
  391.6 0.3 all-gather.8.cloned.1.call-start
  392.1 0.1 clamp_reduce_fusion
  392.3 9.1 %all-to-all-done.1 = f32[32,1,512]{2,1,0:T(1,128)S(1)} async-done(((f32[32,1,512]{2,1,0:T(1,128)}), f32[32,1,512]{2,1,0:T(1,128)S(1)}, u32[]{:S(2)}, u32[]{:S(2)}) %all-to-all-start.1) | async-done | bytes 65568 | tf_op jit(solution)/shard_map/all_to_all | solution.py:95
  401.4 0.7 reduce.25
  402.3 0.1 all_to_all.49
  402.4 14.9 %fusion.50 = f32[2048,8]{0,1:T(8,128)S(1)} fusion(f32[2048,8]{0,1:T(8,128)S(1)} %all_to_all.49, s32[2048]{0:T(1024)S(1)} %min.26, f32[4096,8]{0,1:T(8,128)S(1)} %copy-done.7, f32[4096,8]{0,1:T(8,128)S(1)} %get-tuple-element.132, f32[4096]{0:T(1024)S(1)} %copy-done.9), kind=kOutput, calls=%fused_computation.65 | convolution fusion | flops 813809664 | bytes 417792 | tf_op jit(solution)/shard_map/dot_general | solution.py:101
  417.3 11.6 %fusion.101 = (bf16[4096,8]{0,1:T(8,128)(2,1)}, f32[4096,8]{0,1:T(8,128)S(1)}, f32[4096,8]{0,1:T(8,128)S(1)}) fusion(f32[4096,8]{0,1:T(8,128)S(1)} %get-tuple-element.132, f32[2048,8]{0,1:T(8,128)S(1)} %fusion.50, s32[2048]{0:T(1024)S(1)} %min.26, f32[4096,8]{0,1:T(8,128)S(1)} %get-tuple-element.136), kind=kOutput, calls=%fused_computation.130 | convolution fusion | flops 813858816 | bytes 663552 | tf_op jit(solution)/shard_map/dot_general | solution.py:102
  428.9 0.2 all-reduce.11.cloned.1.call-start
  429.2 2.4 broadcast.121.clone.2
  431.6 8.1 %while.32 = (s32[]{:T(128)}, bf16[2,256,4096]{2,1,0:T(8,128)(2,1)}, bf16[2,64,256]{2,1,0:T(8,128)(2,1)S(1)}, f32[4096]{0:T(1024)S(1)}, bf16[64,4096]{1,0:T(8,128)(2,1)S(1)}, /*index=5*/s32[]{:T(128)}) while((s32[]{:T(128)}, bf16[2,256,4096]{2,1,0:T(8,128)(2,1)}, bf16[2,64,256]{2,1,0:T(8,128)(2,1)S(1)}, f32[4096]{0:T(1024)S(1)}, ...), condition=%wide.region_12.13_spmd, body=%wide.region_10.12_spmd.sunk | while | flops 143703808 | bytes 2706513 | solution.py:81
  431.6 4.1 fusion.147
  435.7 4.0 fusion.147
  439.7 37.7 %all-gather.8.cloned.1.call-done = bf16[4096,256]{0,1:T(8,128)(2,1)} async-done(((bf16[4096,8]{0,1:T(8,128)(2,1)}), bf16[4096,256]{0,1:T(8,128)(2,1)}) %all-gather.8.cloned.1.call-update) | async-done | bytes 2097168 | tf_op jit(solution)/shard_map/all_gather | solution.py:90
  477.4 4.2 fusion.107
  481.6 4.7 fusion.66
  486.3 0.4 reduce-scatter.4.cloned.1.call-start
  486.8 14.6 %convolution_bitcast_fusion = f32[256,2048]{0,1:T(8,128)S(1)} fusion(bf16[512,256]{1,0:T(8,128)(2,1)S(1)} %copy-done, bf16[64,512]{1,0:T(8,128)(2,1)S(1)} %copy-done.8, bf16[64,2048]{1,0:T(8,128)(2,1)S(1)} %copy-done.5, f32[512]{0:T(512)S(1)} %copy-done.10), kind=kOutput, calls=%fused_computation.61 | convolution fusion | flops 674234368 | bytes 2689024 | tf_op jit(solution)/shard_map/dot_general | solution.py:64
  501.4 1.9 copy.37
  503.3 55.5 %all-reduce.11.cloned.1.call-done = f32[512,256]{1,0:T(8,128)} async-done(((f32[512,256]{1,0:T(8,128)}), f32[512,256]{1,0:T(8,128)}) %all-reduce.11.cloned.1.call-update) | async-done | bytes 524304 | tf_op jit(solution)/shard_map/psum | solution.py:93
  558.8 0.8 constant_dynamic-slice_fusion
  559.7 0.8 reshape.129
  560.5 14.0 %all-to-all-start.2 = ((f32[32,1,512]{2,1,0:T(1,128)}), f32[32,1,512]{2,1,0:T(1,128)S(1)}, u32[]{:S(2)}, u32[]{:S(2)}) async-start(f32[32,1,512]{2,1,0:T(1,128)} %reshape.129), calls=%async_computation.2 | async-start | bytes 131072 | tf_op jit(solution)/shard_map/all_to_all | solution.py:95
  574.6 9.7 %all-to-all-done.2 = f32[32,1,512]{2,1,0:T(1,128)S(1)} async-done(((f32[32,1,512]{2,1,0:T(1,128)}), f32[32,1,512]{2,1,0:T(1,128)S(1)}, u32[]{:S(2)}, u32[]{:S(2)}) %all-to-all-start.2) | async-done | bytes 65568 | tf_op jit(solution)/shard_map/all_to_all | solution.py:95
  584.3 0.7 reduce.26
  585.3 14.9 %fusion.51 = f32[2048,8]{0,1:T(8,128)S(1)} fusion(f32[2048,8]{0,1:T(8,128)S(1)} %all_to_all.53, s32[2048]{0:T(1024)S(1)} %min.28, f32[4096,8]{0,1:T(8,128)S(1)} %copy-done.7, f32[4096,8]{0,1:T(8,128)S(1)} %get-tuple-element.130, f32[4096]{0:T(1024)S(1)} %copy-done.9), kind=kOutput, calls=%fused_computation.66 | convolution fusion | flops 813809664 | bytes 417792 | tf_op jit(solution)/shard_map/dot_general | solution.py:101
  600.2 11.5 %fusion.104 = (f32[4096,8]{0,1:T(8,128)}, f32[4096,8]{0,1:T(8,128)}) fusion(f32[4096,8]{0,1:T(8,128)S(1)} %get-tuple-element.130, f32[2048,8]{0,1:T(8,128)S(1)} %fusion.51, s32[2048]{0:T(1024)S(1)} %min.28, f32[4096,8]{0,1:T(8,128)S(1)} %get-tuple-element.137), kind=kOutput, calls=%fused_computation.133 | convolution fusion | flops 813826048 | bytes 598016 | tf_op jit(solution)/shard_map/dot_general | solution.py:102
  611.7 8.4 %reduce-scatter.4.cloned.1.call-done = f32[32,2048]{1,0:T(8,128)} async-done(((f32[256,2048]{1,0:T(8,128)}), f32[32,2048]{1,0:T(8,128)}) %reduce-scatter.4.cloned.1.call-update) | async-done | bytes 262160
  (66 shorter events, 1.8 us)
Async XLA Ops:
  8.0 99.8 %copy-start = (bf16[512,256]{1,0:T(8,128)(2,1)S(1)}, bf16[512,256]{1,0:T(8,128)(2,1)}, u32[]{:S(2)}) copy-start(bf16[512,256]{1,0:T(8,128)(2,1)} %param.23) | copy-start | bytes 786436
  8.0 84.1 %all-reduce.5.cloned.1.call-start = ((), (), s32[]{:S(2)}) async-start(), calls=%async_computation.4 | async-start | bytes 393216 | tf_op jit(solution)/shard_map/psum | solution.py:61
  8.8 6.1 copy-start.4
  8.8 7.0 %copy-start.1 = (bf16[64,4096]{1,0:T(8,128)(2,1)S(1)}, bf16[64,4096]{1,0:T(8,128)(2,1)}, u32[]{:S(2)}) copy-start(bf16[64,4096]{1,0:T(8,128)(2,1)} %param.16) | copy-start | bytes 1572868
  14.9 88.7 %all-gather.4.cloned.1.call-start = ((), (), s32[]{:S(2)}) async-start(), calls=%async_computation.5 | async-start | bytes 2162688 | tf_op jit(solution)/shard_map/all_gather | solution.py:90
  15.6 176.9 %all-reduce.7.cloned.1.call-start = ((), (), s32[]{:S(2)}) async-start(), calls=%async_computation.6 | async-start | bytes 1048576 | tf_op jit(solution)/shard_map/psum | solution.py:93
  103.6 4.3 copy-start.2
  103.6 4.3 copy-start.8
  103.6 4.3 copy-start.10
  103.6 105.0 %copy-start.3 = (s32[3,16384]{1,0:T(4,128)S(1)}, s32[3,16384]{1,0:T(4,128)}, u32[]{:S(2)}) copy-start(s32[3,16384]{1,0:T(4,128)} %param.25) | copy-start | bytes 589828
  107.9 111.7 %copy-start.7 = (f32[4096,8]{0,1:T(8,128)S(1)}, f32[4096,8]{0,1:T(8,128)}, u32[]{:S(2)}) copy-start(f32[4096,8]{0,1:T(8,128)} %param.18) | copy-start | bytes 393220
  107.9 111.7 %copy-start.9 = (f32[4096]{0:T(1024)S(1)}, f32[4096]{0:T(1024)}, u32[]{:S(2)}) copy-start(f32[4096]{0:T(1024)} %param.17) | copy-start | bytes 49156
  194.3 23.8 %all-to-all-start = ((f32[32,1,512]{2,1,0:T(1,128)}), f32[32,1,512]{2,1,0:T(1,128)S(1)}, u32[]{:S(2)}, u32[]{:S(2)}) async-start(f32[32,1,512]{2,1,0:T(1,128)} %reshape.125), calls=%async_computation | async-start | bytes 131072 | tf_op jit(solution)/shard_map/all_to_all | solution.py:95
  208.3 86.3 %all-gather.6.cloned.1.call-start = ((), (), s32[]{:S(2)}) async-start(), calls=%async_computation.7 | async-start | bytes 2162688 | tf_op jit(solution)/shard_map/all_gather | solution.py:90
  219.5 15.4 %copy-start.6 = (f32[4096,8]{0,1:T(8,128)S(1)}, f32[4096,8]{0,1:T(8,128)}, u32[]{:S(2)}) copy-start(f32[4096,8]{0,1:T(8,128)} %param.20) | copy-start | bytes 393220
  246.1 129.8 %all-reduce.9.cloned.1.call-start = ((), (), s32[]{:S(2)}) async-start(), calls=%async_computation.8 | async-start | bytes 1048576 | tf_op jit(solution)/shard_map/psum | solution.py:93
  377.6 23.8 %all-to-all-start.1 = ((f32[32,1,512]{2,1,0:T(1,128)}), f32[32,1,512]{2,1,0:T(1,128)S(1)}, u32[]{:S(2)}, u32[]{:S(2)}) async-start(f32[32,1,512]{2,1,0:T(1,128)} %reshape.127), calls=%async_computation.1 | async-start | bytes 131072 | tf_op jit(solution)/shard_map/all_to_all | solution.py:95
  391.6 85.8 %all-gather.8.cloned.1.call-start = ((), (), s32[]{:S(2)}) async-start(), calls=%async_computation.9 | async-start | bytes 2162688 | tf_op jit(solution)/shard_map/all_gather | solution.py:90
  428.9 129.9 %all-reduce.11.cloned.1.call-start = ((), (), s32[]{:S(2)}) async-start(), calls=%async_computation.10 | async-start | bytes 1048576 | tf_op jit(solution)/shard_map/psum | solution.py:93
  477.4 9.4 %copy-start.5 = (bf16[64,2048]{1,0:T(8,128)(2,1)S(1)}, bf16[64,2048]{1,0:T(8,128)(2,1)}, u32[]{:S(2)}) copy-start(bf16[64,2048]{1,0:T(8,128)(2,1)} %param.24) | copy-start | bytes 786436
  486.3 133.7 %reduce-scatter.4.cloned.1.call-start = ((), (), s32[]{:S(2)}) async-start(), calls=%async_computation.11 | async-start | bytes 2359296
  560.5 23.8 %all-to-all-start.2 = ((f32[32,1,512]{2,1,0:T(1,128)}), f32[32,1,512]{2,1,0:T(1,128)S(1)}, u32[]{:S(2)}, u32[]{:S(2)}) async-start(f32[32,1,512]{2,1,0:T(1,128)} %reshape.129), calls=%async_computation.2 | async-start | bytes 131072 | tf_op jit(solution)/shard_map/all_to_all | solution.py:95
Sparse Core Ops, SparseCore 0:
  15.0 77.0 all-reduce.4
  112.7 79.7 all-reduce.6
  303.6 72.2 all-reduce.8
  486.5 72.2 all-reduce.10
  561.8 58.2 reduce-scatter.3
Sparse Core Ops, SparseCore 1:
  18.8 58.8 all-gather.3
  246.2 48.4 all-gather.5
  429.0 48.4 all-gather.7
where the time goes:
time: 632 us; the launch traced here: 628 us
  waiting for transfers between devices  395 us (62%)
  matrix products  151 us (24%)
  starting transfers between devices  43.8 us (7%)
  local copies, waits for them, and re-layouts  17.4 us (3%)
  between operations  16.1 us (3%)
    psum x3, waiting for transfers between devices, shards(): summed = lax.psum(partial_sum, 'col')  208 us
    psum x1, waiting for transfers between devices, shards(): batch_points = lax.psum(picked.astype(jnp.bfloat16), 'col')  76.1 us
    all_gather x3, waiting for transfers between devices, shards(): coeffs = lax.all_gather(coeffs, 'row', axis=1, tiled=True)  75.5 us
    dot_general x3, matrix products, shards(): row_terms = arrived + jnp.dot(owner_map, point_terms, precision=HIGH)  45.2 us
    all_to_all x3, starting transfers between devices, shards(): lax.all_to_all(owned_rows, 'row', split_axis=1, concat_axis=0, tiled=True)  42.1 us
    dot_general x3, matrix products, shards(): lax.dot_general(owner_map, row_terms, (((0,), (0,)), ((), ())), precision...  34.2 us
    all_to_all x3, waiting for transfers between devices, shards(): lax.all_to_all(owned_rows, 'row', split_axis=1, concat_axis=0, tiled=True)  27.5 us
    dot_general x6, matrix products, kernel_rows(): lax.dot_general(points, x_train, (((0,), (0,)), ((), ())), preferred_elem...  24.1 us
  transfers between devices with their start and end apart: 11, of which 10 were waited for; matrix products, arithmetic and copies ran while one was open for 13% of the time, Pallas kernels for 0%

commit v1 on v0

v1 whole, which is shorter than its diff:
```python
import jax
import jax.numpy as jnp
import numpy as np
from jax import lax
from jax.experimental import pallas as pl
from jax.experimental.pallas import tpu as pltpu
from jax.sharding import PartitionSpec as P

STEPS = 3
NOISE_VAR = 0.25
MOMENTUM = 0.9
STEP_SIZE = 0.5
LENGTH = 1.15
F32 = jnp.float32
BF16 = jnp.bfloat16
PI = float(np.pi)
PI_HIGH = 3.140625
PI_LOW = PI - PI_HIGH
LN2 = float(np.log(2.0))
KAPPA = float(3.0 / LENGTH**2 / np.log(2.0) ** 2)
NN = (((1,), (0,)), ((), ()))
NT = (((1,), (1,)), ((), ()))


def cosine_fit():
    top = (np.pi / 2 + 1e-4) ** 2
    nodes = (np.cos((2 * np.arange(200) + 1) * np.pi / 400) + 1) * top / 2
    fit = np.polynomial.chebyshev.Chebyshev.fit(nodes, np.cos(np.sqrt(nodes)), 5, domain=[0, top])
    return [float(v) for v in fit.convert(kind=np.polynomial.Polynomial).coef]


COS_COEFS = cosine_fit()


def dot(a, b, dims=NN):
    return lax.dot_general(a, b, dims, preferred_element_type=F32)


def scaled_cos(half_arg, factor):
    turns = jnp.round(half_arg * (1.0 / PI))
    h = (half_arg - turns * PI_HIGH) - turns * PI_LOW
    z = h * h
    c = jnp.full_like(z, COS_COEFS[-1])
    for coef in COS_COEFS[-2::-1]:
        c = c * z + coef
    return c * c * (2.0 * factor) - factor


def matern_kernel(p_ref, b_ref, o_ref, *, chunk):
    b = b_ref[...]
    wide = b.astype(F32)
    b_norm = jnp.sum(wide * wide, axis=0, keepdims=True)
    for i in range(0, p_ref.shape[0], chunk):
        p = p_ref[i : i + chunk, :].astype(F32)
        p_norm = jnp.sum(p * p, axis=1, keepdims=True)
        inner = dot((p * -2.0).astype(BF16), b)
        dist = jnp.maximum((inner + p_norm + b_norm) * KAPPA, 1e-30)
        u = dist * lax.rsqrt(dist)
        value = (u * LN2 + 1.0) * jnp.exp2(-u)
        o_ref[i : i + chunk, :] = value.astype(BF16)


def matern(points, others, block=512, chunk=128):
    rows, cols = points.shape[0], others.shape[1]
    return pl.pallas_call(
        lambda *refs: matern_kernel(*refs, chunk=chunk),
        grid=(cols // block,),
        in_specs=[
            pl.BlockSpec((rows, points.shape[1]), lambda i: (0, 0)),
            pl.BlockSpec((others.shape[0], block), lambda i: (0, i)),
        ],
        out_specs=pl.BlockSpec((rows, block), lambda i: (0, i)),
        out_shape=jax.ShapeDtypeStruct((rows, cols), BF16),
        compiler_params=pltpu.CompilerParams(vmem_limit_bytes=24 << 20),
        cost_estimate=pl.CostEstimate(
            flops=12 * rows * cols, bytes_accessed=2 * rows * cols, transcendentals=2 * rows * cols
        ),
        name="matern",
    )(points, others)


def matern_same_kernel(p_ref, b_ref, pid_ref, bid_ref, o_ref, *, chunk):
    b = b_ref[...]
    wide = b.astype(F32)
    b_norm = jnp.sum(wide * wide, axis=0, keepdims=True)
    bid = bid_ref[...]
    for i in range(0, p_ref.shape[0], chunk):
        p = p_ref[i : i + chunk, :].astype(F32)
        p_norm = jnp.sum(p * p, axis=1, keepdims=True)
        inner = dot((p * -2.0).astype(BF16), b)
        dist = jnp.maximum((inner + p_norm + b_norm) * KAPPA, 1e-30)
        u = dist * lax.rsqrt(dist)
        value = (u * LN2 + 1.0) * jnp.exp2(-u)
        same = pid_ref[i : i + chunk, :] == bid
        o_ref[i : i + chunk, :] = (value + jnp.where(same, NOISE_VAR, 0.0)).astype(BF16)


def matern_same(points, others, point_ids, other_ids, block=512, chunk=128):
    rows, cols = points.shape[0], others.shape[1]
    return pl.pallas_call(
        lambda *refs: matern_same_kernel(*refs, chunk=chunk),
        grid=(cols // block,),
        in_specs=[
            pl.BlockSpec((rows, points.shape[1]), lambda i: (0, 0)),
            pl.BlockSpec((others.shape[0], block), lambda i: (0, i)),
            pl.BlockSpec((rows, 1), lambda i: (0, 0)),
            pl.BlockSpec((1, block), lambda i: (0, i)),
        ],
        out_specs=pl.BlockSpec((rows, block), lambda i: (0, i)),
        out_shape=jax.ShapeDtypeStruct((rows, cols), BF16),
        compiler_params=pltpu.CompilerParams(vmem_limit_bytes=24 << 20),
        cost_estimate=pl.CostEstimate(
            flops=14 * rows * cols, bytes_accessed=2 * rows * cols, transcendentals=2 * rows * cols
        ),
        name="matern_same",
    )(points, others, point_ids, other_ids)


def batch_prior_kernel(p_ref, f_ref, ph_ref, w_ref, o_ref, *, factor, chunk):
    freq = f_ref[...] * BF16(0.5)
    half_phase = ph_ref[...] * 0.5
    for i in range(0, p_ref.shape[0], chunk):
        arg = dot(p_ref[i : i + chunk, :], freq) + half_phase
        phi = scaled_cos(arg, factor).astype(BF16)
        o_ref[i : i + chunk, :] = dot(phi, w_ref[...])


def batch_prior(points, frequencies, phases, weights, factor, block=512, chunk=128):
    rows, feats, paths = points.shape[0], frequencies.shape[1], weights.shape[1]
    return pl.pallas_call(
        lambda *refs: batch_prior_kernel(*refs, factor=factor, chunk=chunk),
        grid=(rows // block,),
        in_specs=[
            pl.BlockSpec((block, points.shape[1]), lambda i: (i, 0)),
            pl.BlockSpec(frequencies.shape, lambda i: (0, 0)),
            pl.BlockSpec((1, feats), lambda i: (0, 0)),
            pl.BlockSpec((feats, paths), lambda i: (0, 0)),
        ],
        out_specs=pl.BlockSpec((block, paths), lambda i: (i, 0)),
        out_shape=jax.ShapeDtypeStruct((rows, paths), F32),
        compiler_params=pltpu.CompilerParams(vmem_limit_bytes=24 << 20),
        cost_estimate=pl.CostEstimate(
            flops=24 * rows * feats, bytes_accessed=4 * rows * paths, transcendentals=rows * feats
        ),
        name="batch_prior",
    )(points, frequencies, phases[None, :], weights)


def window_kernel(f_ref, ph_ref, w_ref, x_ref, o_ref, *, factor, chunk):
    freq = f_ref[...] * BF16(0.5)
    half_phase = ph_ref[...] * 0.5
    total = None
    for i in range(0, f_ref.shape[0], chunk):
        arg = dot(freq[i : i + chunk, :], x_ref[...]) + half_phase[i : i + chunk, :]
        phi = scaled_cos(arg, factor).astype(BF16)
        part = dot(w_ref[:, i : i + chunk], phi)
        total = part if total is None else total + part
    o_ref[...] = total


def window_prior(frequencies, phases, weights, x_window, factor, block=256, chunk=128):
    feats, paths, window = frequencies.shape[1], weights.shape[1], x_window.shape[1]
    return pl.pallas_call(
        lambda *refs: window_kernel(*refs, factor=factor, chunk=chunk),
        grid=(window // block,),
        in_specs=[
            pl.BlockSpec((feats, frequencies.shape[0]), lambda i: (0, 0)),
            pl.BlockSpec((feats, 1), lambda i: (0, 0)),
            pl.BlockSpec((paths, feats), lambda i: (0, 0)),
            pl.BlockSpec((x_window.shape[0], block), lambda i: (0, i)),
        ],
        out_specs=pl.BlockSpec((paths, block), lambda i: (0, i)),
        out_shape=jax.ShapeDtypeStruct((paths, window), F32),
        compiler_params=pltpu.CompilerParams(vmem_limit_bytes=24 << 20),
        cost_estimate=pl.CostEstimate(
            flops=24 * feats * window, bytes_accessed=4 * paths * window, transcendentals=feats * window
        ),
        name="window_prior",
    )(frequencies.T, phases[:, None], weights.T, x_window)


def pick_rows_kernel(i_ref, x_ref, o_ref):
    index = i_ref[...]
    high, low = index & 255, index >> 8
    onehot = (lax.broadcasted_iota(jnp.int32, (index.shape[0], 256), 1) == high).astype(F32).astype(BF16)
    total = jnp.zeros(o_ref.shape, F32)
    for part in range(x_ref.shape[1] // 256):
        found = dot(onehot, x_ref[:, part * 256 : (part + 1) * 256], NT)
        total = total + jnp.where(low == part, found, 0.0)
    o_ref[...] = total.astype(BF16)


def pick_rows(index, x_train):
    return pl.pallas_call(
        pick_rows_kernel,
        out_shape=jax.ShapeDtypeStruct((index.shape[0], x_train.shape[0]), BF16),
        name="pick_rows",
    )(index[:, None], x_train)


def pick_cols_kernel(i_ref, x_ref, o_ref):
    index = i_ref[0]
    high, low = index & 255, index >> 8
    onehot = (lax.broadcasted_iota(jnp.int32, (256, index.shape[1]), 0) == high).astype(F32).astype(BF16)
    total = jnp.zeros(o_ref.shape[1:], F32)
    for part in range(x_ref.shape[1] // 256):
        found = dot(x_ref[:, part * 256 : (part + 1) * 256], onehot)
        total = total + jnp.where(low == part, found, 0.0)
    o_ref[0] = total.astype(BF16)


def pick_cols(index, x_train, block=512):
    steps, count = index.shape
    return pl.pallas_call(
        pick_cols_kernel,
        grid=(steps, count // block),
        in_specs=[
            pl.BlockSpec((1, 1, block), lambda t, i: (t, 0, i)),
            pl.BlockSpec(x_train.shape, lambda t, i: (0, 0)),
        ],
        out_specs=pl.BlockSpec((1, x_train.shape[0], block), lambda t, i: (t, 0, i)),
        out_shape=jax.ShapeDtypeStruct((steps, x_train.shape[0], count), BF16),
        compiler_params=pltpu.CompilerParams(vmem_limit_bytes=24 << 20),
        cost_estimate=pl.CostEstimate(
            flops=60 * steps * count * 256, bytes_accessed=1 << 20, transcendentals=0
        ),
        name="pick_cols",
    )(index[:, None, :], x_train)


def spread(index, rows, train):
    high, low = index >> 7, index & 127
    low_hot = (lax.broadcasted_iota(jnp.int32, (128, index.shape[1]), 0) == low).astype(F32).astype(BF16)
    tiles = [jnp.where(high == h, rows, 0.0) for h in range(train // 128)]
    return dot(jnp.concatenate(tiles, axis=0).astype(BF16), low_hot, NT)


def known_kernel(i_ref, t_ref, n_ref, a_ref, v_ref, cnt_ref, a1_ref, a2_ref):
    train = a_ref.shape[1]
    ones = jnp.ones((8, i_ref.shape[1]), F32)
    for t in range(STEPS):
        tiles = spread(i_ref[t : t + 1, :], ones, train)
        for h in range(train // 128):
            cnt_ref[t, :, h * 128 : (h + 1) * 128] = tiles[h * 8 : (h + 1) * 8, :]
    dual, velocity = a_ref[...], v_ref[...]
    fixed = n_ref[...] - t_ref[...]
    for t, out in enumerate((a1_ref, a2_ref)):
        gradient = cnt_ref[t] * (NOISE_VAR * dual + fixed)
        velocity = MOMENTUM * velocity - STEP_SIZE * gradient
        dual = dual + velocity
        out[...] = dual.astype(BF16)


def known_parts(index, targets, noise, dual, velocity):
    shape = dual.shape
    return pl.pallas_call(
        known_kernel,
        out_shape=(
            jax.ShapeDtypeStruct((STEPS,) + shape, F32),
            jax.ShapeDtypeStruct(shape, BF16),
            jax.ShapeDtypeStruct(shape, BF16),
        ),
        compiler_params=pltpu.CompilerParams(vmem_limit_bytes=32 << 20),
        cost_estimate=pl.CostEstimate(flops=1 << 23, bytes_accessed=1 << 20, transcendentals=0),
        name="known_parts",
    )(index, targets[None, :], noise, dual, velocity)


def place_kernel(i_ref, r_ref, o_ref):
    train = o_ref.shape[1]
    tiles = spread(i_ref[...], r_ref[...].astype(F32), train)
    for h in range(train // 128):
        o_ref[:, h * 128 : (h + 1) * 128] = tiles[h * 8 : (h + 1) * 8, :]


def place(index, rows, train):
    return pl.pallas_call(
        place_kernel,
        out_shape=jax.ShapeDtypeStruct((8, train), F32),
        compiler_params=pltpu.CompilerParams(vmem_limit_bytes=32 << 20),
        cost_estimate=pl.CostEstimate(flops=1 << 21, bytes_accessed=1 << 18, transcendentals=0),
        name="place",
    )(index[None, :], rows)


def finish_kernel(i_ref, r_ref, z0_ref, z1_ref, cnt_ref, t_ref, n_ref, a_ref, v_ref, ao_ref, vo_ref):
    train = a_ref.shape[1]
    rows = r_ref[...]
    coarse = rows.astype(BF16).astype(F32)
    tiles = spread(i_ref[...], coarse, train) + spread(i_ref[...], rows - coarse, train)
    dual, velocity = a_ref[...], v_ref[...]
    fixed = n_ref[...] - t_ref[...]
    z0 = z0_ref[...]
    velocity = MOMENTUM * velocity - STEP_SIZE * (z0 + cnt_ref[0] * (NOISE_VAR * dual + fixed))
    first = dual - STEP_SIZE * z0
    known = dual
    dual = dual + velocity
    change = -STEP_SIZE * z0
    gradient = z1_ref[...] + cnt_ref[1] * (NOISE_VAR * (dual - change) + fixed)
    velocity = MOMENTUM * velocity - STEP_SIZE * gradient
    dual = dual + velocity
    base = cnt_ref[2] * (NOISE_VAR * dual + fixed)
    for h in range(train // 128):
        at = slice(h * 128, (h + 1) * 128)
        vo_ref[:, at] = MOMENTUM * velocity[:, at] - STEP_SIZE * (
            base[:, at] + tiles[h * 8 : (h + 1) * 8, :]
        )
    ao_ref[...] = dual + vo_ref[...]


def finish(index, rows, z0, z1, counts, targets, noise, dual, velocity):
    shape = jax.ShapeDtypeStruct(dual.shape, F32)
    return pl.pallas_call(
        finish_kernel,
        out_shape=(shape, shape),
        compiler_params=pltpu.CompilerParams(vmem_limit_bytes=48 << 20),
        cost_estimate=pl.CostEstimate(flops=1 << 22, bytes_accessed=1 << 20, transcendentals=0),
        name="finish",
    )(index[None, :], rows, z0, z1, counts, targets[None, :], noise, dual, velocity)


def row_id_of(x, z, core):
    return (x * 4 + z) * 2 + core


X_GROUPS = [[row_id_of(x, z, c) for x in range(4)] for z in range(4) for c in range(2)]
Z_GROUPS = [[row_id_of(x, z, c) for z in range(4)] for x in range(4) for c in range(2)]
CORE_SWAP = [(i, i ^ 1) for i in range(32)]


def gather_groups(x, groups):
    spread_out = jnp.broadcast_to(x[None], (len(groups[0]),) + x.shape)
    return lax.all_to_all(spread_out, "row", 0, 0, axis_index_groups=groups, tiled=True)


def gather_rows(x, row_id):
    shape = x.shape
    x = gather_groups(x, Z_GROUPS)
    x = gather_groups(x, X_GROUPS)
    other = lax.ppermute(x, "row", CORE_SWAP)
    even = row_id % 2 == 0
    pair = jnp.stack([jnp.where(even, x, other), jnp.where(even, other, x)], axis=2)
    return pair.reshape((32,) + shape)


def shards(
    x_train,
    targets,
    noise_draws,
    alpha_init,
    velocity_init,
    frequencies,
    phases,
    path_weights,
    x_window,
    batch_index,
):
    rows, cols = lax.axis_size("row"), lax.axis_size("col")
    row_id, col_id = lax.axis_index("row"), lax.axis_index("col")
    train = x_train.shape[1]
    batch_rows = batch_index.shape[1] // rows
    own_rows = batch_rows // cols
    group_rows = rows * own_rows
    paths = path_weights.shape[1]
    own_paths = paths // rows
    factor = (2.0 / (frequencies.shape[1] * cols)) ** 0.5
    dual, velocity, noise = alpha_init.T, velocity_init.T, noise_draws.T

    by_group = batch_index.reshape(STEPS, rows, cols, own_rows)
    mine = lax.dynamic_slice_in_dim(by_group, col_id, 1, 2)[:, :, 0] - col_id * train
    group_index = mine.reshape(STEPS, group_rows)
    own_index = lax.dynamic_slice_in_dim(mine, row_id, 1, 1).reshape(STEPS * own_rows)

    own_points = pick_rows(own_index, x_train)
    points = lax.all_to_all(
        jnp.broadcast_to(own_points[None], (cols,) + own_points.shape), "col", 0, 0, tiled=True
    )
    points = points.reshape(cols, STEPS, own_rows, -1).transpose(1, 0, 2, 3)
    points = points.reshape(STEPS, batch_rows, -1)

    gathered0 = gather_rows(dual.astype(BF16), row_id).reshape(paths, train)
    counts, known1, known2 = known_parts(group_index, targets, noise, dual, velocity)
    gathered1 = lax.all_gather(known1, "row", axis=0, tiled=True)
    gathered2 = lax.all_gather(known2, "row", axis=0, tiled=True)

    window_part = window_prior(frequencies, phases, path_weights, x_window, factor)
    prior_window = lax.psum_scatter(window_part, "col", scatter_dimension=0, tiled=True)

    prior = batch_prior(points.reshape(STEPS * batch_rows, -1), frequencies, phases, path_weights, factor)
    prior = prior.reshape(STEPS, batch_rows, paths)
    full = [matern(points[t], x_train) for t in range(STEPS)]
    group_points = pick_cols(group_index[:2], x_train)
    row_index = lax.dynamic_slice_in_dim(batch_index, row_id * batch_rows, batch_rows, 1) - col_id * train
    between10 = matern_same(points[1], group_points[0], row_index[1][:, None], group_index[0][None, :])
    between20 = matern(points[2], group_points[0])
    between21 = matern(points[2], group_points[1])

    def reduce_cols(part):
        blocks = part.astype(BF16).reshape(cols, own_rows, paths)
        blocks = lax.all_to_all(blocks, "col", 0, 0, tiled=True)
        return jnp.sum(blocks.astype(F32), axis=0)

    chooser = lax.broadcasted_iota(jnp.int32, (own_paths, paths), 1)
    chooser = chooser - own_paths * row_id == lax.broadcasted_iota(jnp.int32, (own_paths, paths), 0)
    chooser = chooser.astype(BF16)

    terms0 = reduce_cols(dot(full[0], gathered0, NT) + prior[0]).astype(BF16)
    terms0 = gather_rows(terms0, row_id).reshape(group_rows, paths)
    part1 = dot(full[1], gathered1, NT) + prior[1]
    terms1 = reduce_cols(part1 - STEP_SIZE * dot(between10, terms0)).astype(BF16)
    z0 = place(group_index[0], dot(chooser, terms0, NT), train)
    part2 = dot(full[2], gathered2, NT) + prior[2]
    part2 = part2 - (STEP_SIZE * (1.0 + MOMENTUM)) * dot(between20, terms0)
    terms1 = gather_rows(terms1, row_id).reshape(group_rows, paths)
    terms2 = reduce_cols(part2 - STEP_SIZE * dot(between21, terms1))
    z1 = place(group_index[1], dot(chooser, terms1, NT), train)
    blocks = terms2.T.reshape(rows, own_paths, own_rows)
    blocks = lax.all_to_all(blocks, "row", 0, 0, tiled=True)
    own_terms = blocks.transpose(1, 0, 2).reshape(own_paths, group_rows)
    dual, velocity = finish(
        group_index[2], own_terms, z0, z1, counts, targets, noise, dual, velocity
    )
    return (dual.T, velocity.T, prior_window)


def solution(mesh):
    placed = (
        P(None, "col"),
        P("col"),
        P("col", "row"),
        P("col", "row"),
        P("col", "row"),
        P(None, "col"),
        P("col"),
        P("col", None),
        P(None, "row"),
        P(),
    )
    return jax.shard_map(
        shards,
        mesh=mesh,
        in_specs=placed,
        out_specs=(P("col", "row"), P("col", "row"), P("col", "row")),
        check_vma=False,
    )
```

time: 632 us -> 249 us (0.39)
  waiting for transfers between devices: 395 us -> 35.1 us
  matrix products: 151 us -> 14.7 us
  blocking collectives: 0 us -> 64.3 us
  Pallas kernels: 0 us -> 47.3 us
  local copies, waits for them, and re-layouts: 17.4 us -> 24.8 us
  starting transfers between devices: 43.8 us -> 36.9 us
    psum x4 -> x0, waiting for transfers between devices: 284 us -> none  [the longest x3 208 us: shards(): summed = lax.psum(partial_sum, 'col')]
    dot_general x20 -> x8, matrix products: 151 us -> 14.7 us  [dot(): return lax.dot_general(a, b, dims, preferred_element_type=F32)]
    all_gather x3 -> x2, waiting for transfers between devices: 75.5 us -> 0.01 us  [the longest x1 0.01 us: shards(): gathered1 = lax.all_gather(known1, 'row', axis=0, tiled=True)]
    all_to_all x0 -> x5, blocking collectives: none -> 64.3 us  [the longest x3 41.8 us: gather_groups(): lax.all_to_all(spread_out, 'row', 0, 0, axis_index_groups=groups, tiled=T...]
    pallas_call x0 -> x14, Pallas kernels: none -> 47.3 us  [the longest x5 18.9 us: matern(): pl.pallas_call(lambda *refs: matern_kernel(*refs, chunk=chunk), grid=(col...]
    all_to_all x3 -> x6, starting transfers between devices: 42.1 us -> 27.1 us  [the longest x3 12.7 us: gather_groups(): lax.all_to_all(spread_out, 'row', 0, 0, axis_index_groups=groups, tiled=T...]
    unnamed x32 -> x62, local copies, waits for them, and re-layouts: 4.5 us -> 15.1 us
    ppermute x0 -> x3, starting transfers between devices: none -> 9.69 us  [gather_rows(): other = lax.ppermute(x, 'row', CORE_SWAP)]
  transfers between devices with their start and end apart: 11 -> 12, of which waited for: 10 -> 4; matrix products, arithmetic and copies ran while one was open for 13% -> 13% of each run, Pallas kernels for 0% -> 18%
where the time goes in v1:
time: 249 us; the launch traced here: 247 us
  blocking collectives  64.3 us (26%)
  Pallas kernels  47.3 us (19%)
  starting transfers between devices  36.9 us (15%)
  waiting for transfers between devices  35.1 us (14%)
  local copies, waits for them, and re-layouts  24.8 us (10%)
  between operations  16.1 us (6%)
  matrix products  14.7 us (6%)
  other arithmetic  8.24 us (3%)
    all_to_all x3, blocking collectives, gather_groups(): lax.all_to_all(spread_out, 'row', 0, 0, axis_index_groups=groups, tiled=T...  41.8 us
    all_to_all x2, blocking collectives, reduce_cols(): blocks = lax.all_to_all(blocks, 'col', 0, 0, tiled=True)  22.6 us
    pallas_call x5, Pallas kernels, matern(): pl.pallas_call(lambda *refs: matern_kernel(*refs, chunk=chunk), grid=(col...  18.9 us
    unnamed x62, local copies, waits for them, and re-layouts  15.1 us
    dot_general x8, matrix products, dot(): return lax.dot_general(a, b, dims, preferred_element_type=F32)  14.7 us
    all_to_all x3, starting transfers between devices, gather_groups(): lax.all_to_all(spread_out, 'row', 0, 0, axis_index_groups=groups, tiled=T...  12.7 us
    all_to_all x3, waiting for transfers between devices, gather_groups(): lax.all_to_all(spread_out, 'row', 0, 0, axis_index_groups=groups, tiled=T...  11.5 us
    ppermute x3, starting transfers between devices, gather_rows(): other = lax.ppermute(x, 'row', CORE_SWAP)  9.69 us
  transfers between devices with their start and end apart: 12, of which 4 were waited for; matrix products, arithmetic and copies ran while one was open for 13% of the time, Pallas kernels for 18%

profile of v1, /device:TPU:1, one launch (start us, length us, event | category | flops | bytes accessed | tf_op | source)
XLA Modules:
  0.0 247.4 jit_solution(2735002534889940025)
XLA Ops:
  8.0 1.2 reshape.69
  9.4 0.9 copy-done.1
  10.3 0.9 copy-done.4
  11.2 0.9 copy-done.6
  12.1 0.7 copy-done.12
  12.9 1.9 known_parts.1
  14.8 0.9 bitcast_convert_fusion
  15.7 17.9 %all_to_all.55 = bf16[4,8,4096]{2,1,0:T(8,128)(2,1)S(1)} all-to-all(bf16[4,8,4096]{2,1,0:T(8,128)(2,1)S(1)} %broadcast_in_dim.26), channel_id=1, replica_groups={{0,16,32,48},{8,24,40,56},{64,80,96,112},{72,88,104,120},{128,144,160,1..., dimensions={0} | all-to-all | bytes 524288 | tf_op jit(solution)/shard_map/all_to_all | solution.py:333
  33.6 1.1 broadcast_in_dim.27
  34.7 4.2 %all-to-all-start.2 = ((bf16[4,4,8,4096]{3,2,1,0:T(8,128)(2,1)}), bf16[4,4,8,4096]{3,2,1,0:T(8,128)(2,1)}, u32[]{:S(2)}, u32[]{:S(2)}) async-start(bf16[4,4,8,4096]{3,2,1,0:T(8,128)(2,1)} %broadcast_in_dim.27), calls=%async_computation.2 | async-start | bytes 2097152 | tf_op jit(solution)/shard_map/all_to_all | solution.py:333
  39.7 11.5 %all-to-all-done.2 = bf16[4,4,8,4096]{3,2,1,0:T(8,128)(2,1)} async-done(((bf16[4,4,8,4096]{3,2,1,0:T(8,128)(2,1)}), bf16[4,4,8,4096]{3,2,1,0:T(8,128)(2,1)}, u32[]{:S(2)}, u32[]{:S(2)}) %all-to-all-start.2) | async-done | bytes 1048608 | tf_op jit(solution)/shard_map/all_to_all | solution.py:333
  51.2 4.1 %collective-permute-start = (bf16[4,4,8,4096]{3,2,1,0:T(8,128)(2,1)}, bf16[4,4,8,4096]{3,2,1,0:T(8,128)(2,1)}, u32[]{:S(2)}, u32[]{:S(2)}) collective-permute-start(bf16[4,4,8,4096]{3,2,1,0:T(8,128)(2,1)} %all-to-all-done.2), channel_id=1, source_target_pairs={{0,8},{8,0},{16,24},{24,16},{32,40},{40,32},{48,56},{56,48},{64,72... | collective-permute-start | bytes 3145736 | tf_op jit(solution)/shard_map/ppermute | solution.py:340
  55.3 0.8 broadcast_in_dim_reshape.4.i_ref
  56.1 2.3 pick_rows.1
  58.4 0.9 copy.31
  59.3 0.7 broadcast_in_dim.22
  60.0 5.0 %all-to-all-start = ((bf16[8,192,64]{1,2,0:T(8,128)(2,1)}), bf16[8,192,64]{1,2,0:T(8,128)(2,1)S(1)}, u32[]{:S(2)}, u32[]{:S(2)}) async-start(bf16[8,192,64]{1,2,0:T(8,128)(2,1)} %broadcast_in_dim.22), calls=%async_computation | async-start | bytes 524288 | tf_op jit(solution)/shard_map/all_to_all | solution.py:375
  65.0 9.1 %all-to-all-done = bf16[8,192,64]{1,2,0:T(8,128)(2,1)S(1)} async-done(((bf16[8,192,64]{1,2,0:T(8,128)(2,1)}), bf16[8,192,64]{1,2,0:T(8,128)(2,1)S(1)}, u32[]{:S(2)}, u32[]{:S(2)}) %all-to-all-start) | async-done | bytes 196640 | tf_op jit(solution)/shard_map/all_to_all | solution.py:375
  74.5 0.7 copy-done.26
  75.2 3.4 %batch_prior.1 = f32[1536,256]{1,0:T(8,128)S(1)} custom-call(bf16[1536,64]{1,0:T(8,128)(2,1)S(1)} %bitcast.73, bf16[64,512]{1,0:T(8,128)(2,1)S(1)} %copy-done.9, f32[1,512]{1,0:T(1,128)S(1)} %bitcast.90, bf16[512,256]{1,0:T(8,128)(2,1)S(1)} %copy-done.3), custom_call_target="tpu_custom_call" | custom-call | flops 18874368 | bytes 1572864 | tf_op jit(solution)/shard_map/batch_prior/pallas_call | solution.py:130
  78.6 0.7 fusion.11
  79.3 4.7 %matern.7 = bf16[512,4096]{1,0:T(8,128)(2,1)S(1)} custom-call(bf16[512,64]{1,0:T(8,128)(2,1)S(1)} %bitcast.87, bf16[64,4096]{1,0:T(8,128)(2,1)S(1)} %copy-done), custom_call_target="tpu_custom_call" | custom-call | flops 25165824 | bytes 4194304 | tf_op jit(solution)/shard_map/matern/pallas_call | solution.py:65
  84.0 1.7 select_bitcast_fusion.1
  85.9 1.3 fusion.5
  87.2 9.3 %all_to_all.56 = bf16[8,64,256]{2,1,0:T(8,128)(2,1)S(1)} all-to-all(bf16[8,64,256]{2,1,0:T(8,128)(2,1)S(1)} %bitcast.103), channel_id=1, replica_groups=mesh['row'=32,'col'=8] {'col'}, dimensions={0} | all-to-all | bytes 524288 | tf_op jit(solution)/shard_map/all_to_all | solution.py:400
  96.6 10.8 %all_to_all.57 = bf16[4,64,256]{2,1,0:T(8,128)(2,1)S(1)} all-to-all(bf16[4,64,256]{2,1,0:T(8,128)(2,1)S(1)} %broadcast_in_dim.28), channel_id=1, replica_groups={{0,16,32,48},{8,24,40,56},{64,80,96,112},{72,88,104,120},{128,144,160,1..., dimensions={0} | all-to-all | bytes 262144 | tf_op jit(solution)/shard_map/all_to_all | solution.py:333
  107.4 0.8 broadcast_in_dim.29
  108.2 4.4 %all-to-all-start.5 = ((bf16[4,4,64,256]{3,2,1,0:T(8,128)(2,1)}), bf16[4,4,64,256]{3,2,1,0:T(8,128)(2,1)}, u32[]{:S(2)}, u32[]{:S(2)}) async-start(bf16[4,4,64,256]{3,2,1,0:T(8,128)(2,1)} %broadcast_in_dim.29), calls=%async_computation.5 | async-start | bytes 1048576 | tf_op jit(solution)/shard_map/all_to_all | solution.py:333
  113.1 8.3 %window_prior.1 = f32[256,2048]{1,0:T(8,128)} custom-call(bf16[512,64]{1,0:T(8,128)(2,1)S(1)} %bitcast.81, f32[512,1]{1,0:T(8,128)S(1)} %copy.44.refs_1_, bf16[256,512]{1,0:T(8,128)(2,1)S(1)} %bitcast.76, bf16[64,2048]{1,0:T(8,128)(2,1)S(1)} %copy-done.8), custom_call_target="tpu_custom_call" | custom-call | flops 25165824 | bytes 2097152 | tf_op jit(solution)/shard_map/window_prior/pallas_call | solution.py:163
  122.0 3.3 %collective-permute-start.1 = (bf16[4,4,64,256]{3,2,1,0:T(8,128)(2,1)}, bf16[4,4,64,256]{3,2,1,0:T(8,128)(2,1)}, u32[]{:S(2)}, u32[]{:S(2)}) collective-permute-start(bf16[4,4,64,256]{3,2,1,0:T(8,128)(2,1)} %all-to-all-done.5), channel_id=1, source_target_pairs={{0,8},{8,0},{16,24},{24,16},{32,40},{40,32},{48,56},{56,48},{64,72... | collective-permute-start | bytes 1572872 | tf_op jit(solution)/shard_map/ppermute | solution.py:340
  125.3 0.8 fusion.10
  126.4 7.0 %pick_cols.1 = bf16[2,64,2048]{2,1,0:T(8,128)(2,1)S(1)} custom-call(s32[2,1,2048]{2,1,0:T(1,128)S(1)} %broadcast_in_dim.25.i_ref, bf16[64,4096]{1,0:T(8,128)(2,1)S(1)} %copy-done), custom_call_target="tpu_custom_call" | custom-call | flops 62914560 | bytes 1048576 | tf_op jit(solution)/shard_map/pick_cols/pallas_call | solution.py:214
  133.5 2.9 %matern_same.1 = bf16[512,2048]{1,0:T(8,128)(2,1)S(1)} custom-call(bf16[512,64]{1,0:T(8,128)(2,1)S(1)} %bitcast.85, bf16[64,2048]{1,0:T(8,128)(2,1)S(1)} %get-tuple-element.23.refs_1_, s32[512,1]{1,0:T(8,128)S(1)} %copy.38.refs_2_, s32[1,2048]{1,0:T(1,128)S(1)} %slice.77.refs_3_.i_ref), custom_call_target="tpu_custom_call" | custom-call | flops 14680064 | bytes 2097152 | tf_op jit(solution)/shard_map/matern_same/pallas_call | solution.py:100
  136.4 1.3 copy-done.21
  137.7 4.7 %matern.9 = bf16[512,4096]{1,0:T(8,128)(2,1)S(1)} custom-call(bf16[512,64]{1,0:T(8,128)(2,1)S(1)} %bitcast.86, bf16[64,4096]{1,0:T(8,128)(2,1)S(1)} %copy-done), custom_call_target="tpu_custom_call" | custom-call | flops 25165824 | bytes 4194304 | tf_op jit(solution)/shard_map/matern/pallas_call | solution.py:65
  142.5 2.0 copy-done.17
  144.4 1.3 select_bitcast_fusion.5
  145.7 1.1 pad_maximum_fusion.1
  146.8 4.3 %convolution_add_fusion = f32[512,256]{1,0:T(8,128)S(1)} fusion(bf16[512,4096]{1,0:T(8,128)(2,1)} %copy-done.17, bf16[256,4096]{1,0:T(8,128)(2,1)} %all-gather.5.cloned.1.call-done, f32[1536,256]{1,0:T(8,128)S(1)} %batch_prior.1), kind=kOutput, calls=%fused_computation.7 | convolution fusion | flops 1073872896 | bytes 7340032 | tf_op jit(solution)/shard_map/dot_general | solution.py:36
  151.1 0.7 fusion.3
  151.9 13.2 %all_to_all.58 = bf16[8,64,256]{2,1,0:T(8,128)(2,1)S(1)} all-to-all(bf16[8,64,256]{2,1,0:T(8,128)(2,1)S(1)} %bitcast.104), channel_id=1, replica_groups=mesh['row'=32,'col'=8] {'col'}, dimensions={0} | all-to-all | bytes 524288 | tf_op jit(solution)/shard_map/all_to_all | solution.py:400
  165.2 13.1 %all_to_all.59 = bf16[4,64,256]{2,1,0:T(8,128)(2,1)S(1)} all-to-all(bf16[4,64,256]{2,1,0:T(8,128)(2,1)S(1)} %broadcast_in_dim.30), channel_id=1, replica_groups={{0,16,32,48},{8,24,40,56},{64,80,96,112},{72,88,104,120},{128,144,160,1..., dimensions={0} | all-to-all | bytes 262144 | tf_op jit(solution)/shard_map/all_to_all | solution.py:333
  178.3 0.9 broadcast_in_dim.31
  179.1 4.1 %all-to-all-start.8 = ((bf16[4,4,64,256]{3,2,1,0:T(8,128)(2,1)}), bf16[4,4,64,256]{3,2,1,0:T(8,128)(2,1)}, u32[]{:S(2)}, u32[]{:S(2)}) async-start(bf16[4,4,64,256]{3,2,1,0:T(8,128)(2,1)} %broadcast_in_dim.31), calls=%async_computation.8 | async-start | bytes 1048576 | tf_op jit(solution)/shard_map/all_to_all | solution.py:333
  183.3 2.4 matern.6
  185.7 1.3 copy-done.15
  187.1 2.4 matern.8
  189.4 1.4 copy-done.19
  190.8 4.7 %matern.5 = bf16[512,4096]{1,0:T(8,128)(2,1)S(1)} custom-call(bf16[512,64]{1,0:T(8,128)(2,1)S(1)} %bitcast.84, bf16[64,4096]{1,0:T(8,128)(2,1)S(1)} %copy-done), custom_call_target="tpu_custom_call" | custom-call | flops 25165824 | bytes 4194304 | tf_op jit(solution)/shard_map/matern/pallas_call | solution.py:65
  195.5 2.0 copy-done.18
  197.5 2.3 collective-permute-start.2
  199.9 4.3 %convolution_add_fusion.2 = f32[512,256]{1,0:T(8,128)S(1)} fusion(bf16[512,4096]{1,0:T(8,128)(2,1)} %copy-done.18, bf16[256,4096]{1,0:T(8,128)(2,1)} %all-gather.3.cloned.1.call-done, f32[1536,256]{1,0:T(8,128)S(1)} %batch_prior.1), kind=kOutput, calls=%fused_computation.9 | convolution fusion | flops 1073872896 | bytes 7340032 | tf_op jit(solution)/shard_map/dot_general | solution.py:36
  204.2 0.7 fusion.2
  204.9 1.3 select_bitcast_fusion.3
  206.4 1.7 copy-done.20
  208.2 1.4 fusion.4
  209.6 3.4 %all-to-all-start.9 = ((bf16[8,64,256]{2,1,0:T(8,128)(2,1)}), bf16[8,64,256]{2,1,0:T(8,128)(2,1)S(1)}, u32[]{:S(2)}, u32[]{:S(2)}) async-start(bf16[8,64,256]{2,1,0:T(8,128)(2,1)} %bitcast.28), calls=%async_computation.9 | async-start | bytes 524288 | tf_op jit(solution)/shard_map/all_to_all | solution.py:400
  214.1 6.0 %all-to-all-done.9 = bf16[8,64,256]{2,1,0:T(8,128)(2,1)S(1)} async-done(((bf16[8,64,256]{2,1,0:T(8,128)(2,1)}), bf16[8,64,256]{2,1,0:T(8,128)(2,1)S(1)}, u32[]{:S(2)}, u32[]{:S(2)}) %all-to-all-start.9) | async-done | bytes 262176 | tf_op jit(solution)/shard_map/all_to_all | solution.py:400
  220.2 0.8 reshape.93
  221.0 6.0 %all-to-all-start.10 = ((f32[32,1,512]{2,1,0:T(1,128)}), f32[32,1,512]{2,1,0:T(1,128)S(1)}, u32[]{:S(2)}, u32[]{:S(2)}) async-start(f32[32,1,512]{2,1,0:T(1,128)} %reshape.93), calls=%async_computation.10 | async-start | bytes 131072 | tf_op jit(solution)/shard_map/all_to_all | solution.py:418
  226.9 1.6 fusion.6.r_ref
  229.1 7.7 %all-to-all-done.10 = f32[32,1,512]{2,1,0:T(1,128)S(1)} async-done(((f32[32,1,512]{2,1,0:T(1,128)}), f32[32,1,512]{2,1,0:T(1,128)S(1)}, u32[]{:S(2)}, u32[]{:S(2)}) %all-to-all-start.10) | async-done | bytes 65568 | tf_op jit(solution)/shard_map/all_to_all | solution.py:418
  237.3 0.8 reduce.14
  238.3 1.6 finish.1
  (98 shorter events, 5.7 us)
Async XLA Ops:
  8.0 138.8 %all-gather.5.cloned.1.call-start = ((), (), s32[]{:S(2)}) async-start(), calls=%async_computation.13 | async-start | bytes 2162688 | tf_op jit(solution)/shard_map/all_gather | solution.py:383
  9.4 0.9 copy-start.1
  10.3 0.9 copy-start.4
  11.2 0.9 copy-start.6
  12.1 0.7 copy-start.12
  34.7 16.5 %all-to-all-start.2 = ((bf16[4,4,8,4096]{3,2,1,0:T(8,128)(2,1)}), bf16[4,4,8,4096]{3,2,1,0:T(8,128)(2,1)}, u32[]{:S(2)}, u32[]{:S(2)}) async-start(bf16[4,4,8,4096]{3,2,1,0:T(8,128)(2,1)} %broadcast_in_dim.27), calls=%async_computation.2 | async-start | bytes 2097152 | tf_op jit(solution)/shard_map/all_to_all | solution.py:333
  38.9 36.3 %copy-start.3 = (bf16[512,256]{1,0:T(8,128)(2,1)S(1)}, bf16[512,256]{1,0:T(8,128)(2,1)}, u32[]{:S(2)}) copy-start(bf16[512,256]{1,0:T(8,128)(2,1)} %refs_3_.2) | copy-start | bytes 786436
  38.9 36.2 %copy-start.9 = (bf16[64,512]{1,0:T(8,128)(2,1)S(1)}, bf16[64,512]{1,0:T(8,128)(2,1)}, u32[]{:S(2)}) copy-start(bf16[64,512]{1,0:T(8,128)(2,1)} %refs_1_.5) | copy-start | bytes 196612
  38.9 36.2 %copy-start.14 = (f32[512]{0:T(512)S(1)}, f32[512]{0:T(512)}, u32[]{:S(2)}) copy-start(f32[512]{0:T(512)} %param.16) | copy-start | bytes 6148
  39.0 160.9 %all-gather.3.cloned.1.call-start = ((), (), s32[]{:S(2)}) async-start(), calls=%async_computation.12 | async-start | bytes 2162688 | tf_op jit(solution)/shard_map/all_gather | solution.py:384
  51.2 32.8 %collective-permute-start = (bf16[4,4,8,4096]{3,2,1,0:T(8,128)(2,1)}, bf16[4,4,8,4096]{3,2,1,0:T(8,128)(2,1)}, u32[]{:S(2)}, u32[]{:S(2)}) collective-permute-start(bf16[4,4,8,4096]{3,2,1,0:T(8,128)(2,1)} %all-to-all-done.2), channel_id=1, source_target_pairs={{0,8},{8,0},{16,24},{24,16},{32,40},{40,32},{48,56},{56,48},{64,72... | collective-permute-start | bytes 3145736 | tf_op jit(solution)/shard_map/ppermute | solution.py:340
  60.0 14.2 %all-to-all-start = ((bf16[8,192,64]{1,2,0:T(8,128)(2,1)}), bf16[8,192,64]{1,2,0:T(8,128)(2,1)S(1)}, u32[]{:S(2)}, u32[]{:S(2)}) async-start(bf16[8,192,64]{1,2,0:T(8,128)(2,1)} %broadcast_in_dim.22), calls=%async_computation | async-start | bytes 524288 | tf_op jit(solution)/shard_map/all_to_all | solution.py:375
  74.4 0.8 copy-start.26
  74.4 4.9 %copy-start = (bf16[64,4096]{1,0:T(8,128)(2,1)S(1)}, bf16[64,4096]{1,0:T(8,128)(2,1)}, u32[]{:S(2)}) copy-start(bf16[64,4096]{1,0:T(8,128)(2,1)} %refs_1_.7) | copy-start | bytes 1572868
  75.2 3.4 %copy-start.27 = (bf16[8,192,64]{2,1,0:T(8,128)(2,1)S(1)}, bf16[8,192,64]{2,1,0:T(8,128)(2,1)}, u32[]{:S(2)}) copy-start(bf16[8,192,64]{2,1,0:T(8,128)(2,1)} %copy-done.26) | copy-start | bytes 589828
  87.2 25.8 %copy-start.8 = (bf16[64,2048]{1,0:T(8,128)(2,1)S(1)}, bf16[64,2048]{1,0:T(8,128)(2,1)}, u32[]{:S(2)}) copy-start(bf16[64,2048]{1,0:T(8,128)(2,1)} %refs_3_.3) | copy-start | bytes 786436
  108.2 13.8 %all-to-all-start.5 = ((bf16[4,4,64,256]{3,2,1,0:T(8,128)(2,1)}), bf16[4,4,64,256]{3,2,1,0:T(8,128)(2,1)}, u32[]{:S(2)}, u32[]{:S(2)}) async-start(bf16[4,4,64,256]{3,2,1,0:T(8,128)(2,1)} %broadcast_in_dim.29), calls=%async_computation.5 | async-start | bytes 1048576 | tf_op jit(solution)/shard_map/all_to_all | solution.py:333
  112.6 127.3 %reduce-scatter.2.cloned.1.call-start = ((), (), s32[]{:S(2)}) async-start(), calls=%async_computation.14 | async-start | bytes 2359296 | tf_op jit(solution)/shard_map/reduce_scatter | solution.py:387
  121.3 12.2 %copy-start.11 = (bf16[1,8,64,64]{3,2,0,1:T(8,128)(2,1)S(1)}, bf16[1,8,64,64]{3,2,0,1:T(8,128)(2,1)}, u32[]{:S(2)}) copy-start(bf16[1,8,64,64]{3,2,0,1:T(8,128)(2,1)} %get-tuple-element.24) | copy-start | bytes 196612
  122.0 22.4 %collective-permute-start.1 = (bf16[4,4,64,256]{3,2,1,0:T(8,128)(2,1)}, bf16[4,4,64,256]{3,2,1,0:T(8,128)(2,1)}, u32[]{:S(2)}, u32[]{:S(2)}) collective-permute-start(bf16[4,4,64,256]{3,2,1,0:T(8,128)(2,1)} %all-to-all-done.5), channel_id=1, source_target_pairs={{0,8},{8,0},{16,24},{24,16},{32,40},{40,32},{48,56},{56,48},{64,72... | collective-permute-start | bytes 1572872 | tf_op jit(solution)/shard_map/ppermute | solution.py:340
  136.4 1.4 copy-start.21
  142.4 2.0 copy-start.17
  146.8 4.3 %copy-start.22 = (bf16[512,2048]{1,0:T(8,128)(2,1)S(1)}, bf16[512,2048]{1,0:T(8,128)(2,1)}, u32[]{:S(2)}) copy-start(bf16[512,2048]{1,0:T(8,128)(2,1)} %copy-done.21) | copy-start | bytes 6291460
  146.8 4.3 %copy-start.23 = (bf16[4,4,2,64,256]{4,3,2,1,0:T(8,128)(2,1)S(1)}, bf16[4,4,2,64,256]{4,3,2,1,0:T(8,128)(2,1)}, u32[]{:S(2)}) copy-start(bf16[4,4,2,64,256]{4,3,2,1,0:T(8,128)(2,1)} %pad_maximum_fusion.1) | copy-start | bytes 3145732
  151.8 31.4 %copy-start.10 = (bf16[1,8,64,64]{3,2,0,1:T(8,128)(2,1)S(1)}, bf16[1,8,64,64]{3,2,0,1:T(8,128)(2,1)}, u32[]{:S(2)}) copy-start(bf16[1,8,64,64]{3,2,0,1:T(8,128)(2,1)} %get-tuple-element.26) | copy-start | bytes 196612
  179.1 18.4 %all-to-all-start.8 = ((bf16[4,4,64,256]{3,2,1,0:T(8,128)(2,1)}), bf16[4,4,64,256]{3,2,1,0:T(8,128)(2,1)}, u32[]{:S(2)}, u32[]{:S(2)}) async-start(bf16[4,4,64,256]{3,2,1,0:T(8,128)(2,1)} %broadcast_in_dim.31), calls=%async_computation.8 | async-start | bytes 1048576 | tf_op jit(solution)/shard_map/all_to_all | solution.py:333
  185.7 1.4 copy-start.15
  189.4 1.4 copy-start.19
  195.5 2.0 copy-start.18
  197.5 6.6 %copy-start.24 = (bf16[4,4,2,64,256]{4,3,2,1,0:T(8,128)(2,1)S(1)}, bf16[4,4,2,64,256]{4,3,2,1,0:T(8,128)(2,1)}, u32[]{:S(2)}) copy-start(bf16[4,4,2,64,256]{4,3,2,1,0:T(8,128)(2,1)} %pad_maximum_fusion.1) | copy-start | bytes 3145732
  197.5 7.4 %collective-permute-start.2 = (bf16[4,4,64,256]{3,2,1,0:T(8,128)(2,1)}, bf16[4,4,64,256]{3,2,1,0:T(8,128)(2,1)}, u32[]{:S(2)}, u32[]{:S(2)}) collective-permute-start(bf16[4,4,64,256]{3,2,1,0:T(8,128)(2,1)} %all-to-all-done.8), channel_id=1, source_target_pairs={{0,8},{8,0},{16,24},{24,16},{32,40},{40,32},{48,56},{56,48},{64,72... | collective-permute-start | bytes 1572872 | tf_op jit(solution)/shard_map/ppermute | solution.py:340
  199.9 4.3 %copy-start.16 = (bf16[512,2048]{1,0:T(8,128)(2,1)S(1)}, bf16[512,2048]{1,0:T(8,128)(2,1)}, u32[]{:S(2)}) copy-start(bf16[512,2048]{1,0:T(8,128)(2,1)} %copy-done.15) | copy-start | bytes 6291460
  206.2 2.0 copy-start.20
  206.4 3.2 %copy-start.25 = (bf16[4,4,2,64,256]{4,3,2,1,0:T(8,128)(2,1)}, bf16[4,4,2,64,256]{4,3,2,1,0:T(8,128)(2,1)S(1)}, u32[]{:S(2)}) copy-start(bf16[4,4,2,64,256]{4,3,2,1,0:T(8,128)(2,1)S(1)} %copy.39) | copy-start | bytes 3145732
  208.2 4.8 %copy-start.28 = (s32[32,64]{1,0:T(8,128)S(1)}, s32[32,64]{1,0:T(8,128)}, u32[]{:S(2)}) copy-start(s32[32,64]{1,0:T(8,128)} %get-tuple-element.13) | copy-start | bytes 24580
  209.6 10.5 %all-to-all-start.9 = ((bf16[8,64,256]{2,1,0:T(8,128)(2,1)}), bf16[8,64,256]{2,1,0:T(8,128)(2,1)S(1)}, u32[]{:S(2)}, u32[]{:S(2)}) async-start(bf16[8,64,256]{2,1,0:T(8,128)(2,1)} %bitcast.28), calls=%async_computation.9 | async-start | bytes 524288 | tf_op jit(solution)/shard_map/all_to_all | solution.py:400
  213.2 25.1 %copy-start.2 = (f32[4096,8]{0,1:T(8,128)S(1)}, f32[4096,8]{0,1:T(8,128)}, u32[]{:S(2)}) copy-start(f32[4096,8]{0,1:T(8,128)} %param.13) | copy-start | bytes 393220
  213.2 25.1 %copy-start.5 = (f32[4096,8]{0,1:T(8,128)S(1)}, f32[4096,8]{0,1:T(8,128)}, u32[]{:S(2)}) copy-start(f32[4096,8]{0,1:T(8,128)} %param.12) | copy-start | bytes 393220
  213.2 25.1 %copy-start.7 = (f32[4096,8]{0,1:T(8,128)S(1)}, f32[4096,8]{0,1:T(8,128)}, u32[]{:S(2)}) copy-start(f32[4096,8]{0,1:T(8,128)} %param.14) | copy-start | bytes 393220
  213.2 25.1 %copy-start.13 = (f32[4096]{0:T(1024)S(1)}, f32[4096]{0:T(1024)}, u32[]{:S(2)}) copy-start(f32[4096]{0:T(1024)} %param.11) | copy-start | bytes 49156
  221.0 15.8 %all-to-all-start.10 = ((f32[32,1,512]{2,1,0:T(1,128)}), f32[32,1,512]{2,1,0:T(1,128)S(1)}, u32[]{:S(2)}, u32[]{:S(2)}) async-start(f32[32,1,512]{2,1,0:T(1,128)} %reshape.93), calls=%async_computation.10 | async-start | bytes 131072 | tf_op jit(solution)/shard_map/all_to_all | solution.py:418
Sparse Core Ops, SparseCore 0:
  14.9 59.4 all-gather.4
  77.0 52.2 all-gather.2
Sparse Core Ops, SparseCore 1:
  121.4 57.8 reduce-scatter.1

commit v2 on v1

v2 whole, which is shorter than its diff:
```python
import jax
import jax.numpy as jnp
import numpy as np
from jax import lax
from jax.experimental import pallas as pl
from jax.experimental.pallas import tpu as pltpu
from jax.sharding import PartitionSpec as P

STEPS = 3
NOISE_VAR = 0.25
MOMENTUM = 0.9
STEP_SIZE = 0.5
LENGTH = 1.15
F32 = jnp.float32
BF16 = jnp.bfloat16
SCALE = float(np.sqrt(3.0) / LENGTH)
LOG2_E = float(1.0 / np.log(2.0))
NN = (((1,), (0,)), ((), ()))
NT = (((1,), (1,)), ((), ()))


def cosine_fit(factor):
    top = 0.2501
    nodes = (np.cos((2 * np.arange(200) + 1) * np.pi / 400) + 1) * top / 2
    wanted = np.sqrt(2.0 * factor) * np.cos(np.pi * np.sqrt(nodes))
    fit = np.polynomial.chebyshev.Chebyshev.fit(nodes, wanted, 5, domain=[0, top])
    return [float(v) for v in fit.convert(kind=np.polynomial.Polynomial).coef]


def dot(a, b, dims=NN):
    return lax.dot_general(a, b, dims, preferred_element_type=F32)


def scaled_cos(half_arg, factor):
    coefs = cosine_fit(factor)
    turns = half_arg * (1.0 / np.pi)
    f = turns - jnp.round(turns)
    z = f * f
    c = z * coefs[-1] + coefs[-2]
    for coef in coefs[-3::-1]:
        c = c * z + coef
    return c * c - factor


def matern_of(dist_sq):
    dist_sq = jnp.maximum(dist_sq, 1e-30)
    dist = dist_sq * lax.rsqrt(dist_sq)
    return (dist * SCALE + 1.0) * jnp.exp2(dist * (-SCALE * LOG2_E))


def three_parts(x):
    high = x.astype(BF16).astype(F32)
    middle = (x - high).astype(BF16).astype(F32)
    return high, middle, x - high - middle


def wide_columns(body, first, second):
    cols = body.shape[1]
    row = lax.broadcasted_iota(jnp.int32, (16, cols), 0)
    high, middle, low = three_parts(second)
    extra = jnp.where(row < 3, first, 0.0)
    extra = jnp.where(row == 3, high, extra)
    extra = jnp.where(row == 4, middle, extra)
    extra = jnp.where(row == 5, low, extra)
    return jnp.concatenate(
        [body.astype(BF16), extra.astype(BF16), jnp.zeros((48, cols), BF16)], axis=0
    )


def distance_columns(b):
    return wide_columns(b * -2.0, 1.0, jnp.sum(b * b, axis=0, keepdims=True))


def setup_kernel(i_ref, x_ref, f_ref, ph_ref, p_ref, xo_ref, fo_ref):
    index = i_ref[...]
    high, low = index & 255, index >> 8
    onehot = (lax.broadcasted_iota(jnp.int32, (index.shape[0], 256), 1) == high).astype(F32).astype(BF16)
    total = jnp.zeros((index.shape[0], x_ref.shape[0]), F32)
    for part in range(x_ref.shape[1] // 256):
        found = dot(onehot, x_ref[:, part * 256 : (part + 1) * 256], NT)
        total = total + jnp.where(low == part, found, 0.0)
    high, middle, low = three_parts(jnp.sum(total * total, axis=1, keepdims=True))
    lane = lax.broadcasted_iota(jnp.int32, total.shape, 1)
    extra = jnp.where(lane < 6, 1.0, 0.0)
    extra = jnp.where(lane == 0, high, extra)
    extra = jnp.where(lane == 1, middle, extra)
    extra = jnp.where(lane == 2, low, extra)
    p_ref[:, :64] = total.astype(BF16)
    p_ref[:, 64:] = extra.astype(BF16)
    for at in range(0, x_ref.shape[1], 512):
        xo_ref[:, at : at + 512] = distance_columns(x_ref[:, at : at + 512].astype(F32))
    fo_ref[...] = wide_columns(f_ref[...].astype(F32) * 0.5, 0.0, ph_ref[...] * 0.5)


def setup(index, x_train, frequencies, phases):
    return pl.pallas_call(
        setup_kernel,
        out_shape=(
            jax.ShapeDtypeStruct((index.shape[0], 128), BF16),
            jax.ShapeDtypeStruct((128, x_train.shape[1]), BF16),
            jax.ShapeDtypeStruct((128, frequencies.shape[1]), BF16),
        ),
        compiler_params=pltpu.CompilerParams(vmem_limit_bytes=24 << 20),
        cost_estimate=pl.CostEstimate(flops=1 << 22, bytes_accessed=2 << 20, transcendentals=0),
        name="setup",
    )(index[:, None], x_train, frequencies, phases[None, :])


def pick_cols_kernel(i_ref, x_ref, o_ref):
    index = i_ref[0]
    high, low = index & 255, index >> 8
    onehot = (lax.broadcasted_iota(jnp.int32, (256, index.shape[1]), 0) == high).astype(F32).astype(BF16)
    parts = x_ref.shape[1] // 256
    stacked = jnp.concatenate([x_ref[:, k * 256 : (k + 1) * 256] for k in range(parts)], axis=0)
    found = dot(stacked, onehot)
    total = jnp.zeros((x_ref.shape[0], index.shape[1]), F32)
    for k in range(parts):
        total = total + jnp.where(low == k, found[k * 64 : (k + 1) * 64], 0.0)
    o_ref[0] = distance_columns(total)


def pick_cols(index, x_train, block=512):
    steps, count = index.shape
    return pl.pallas_call(
        pick_cols_kernel,
        grid=(steps, count // block),
        in_specs=[
            pl.BlockSpec((1, 1, block), lambda t, i: (t, 0, i)),
            pl.BlockSpec(x_train.shape, lambda t, i: (0, 0)),
        ],
        out_specs=pl.BlockSpec((1, 128, block), lambda t, i: (t, 0, i)),
        out_shape=jax.ShapeDtypeStruct((steps, 128, count), BF16),
        compiler_params=pltpu.CompilerParams(vmem_limit_bytes=24 << 20),
        cost_estimate=pl.CostEstimate(
            flops=60 * steps * count * 256, bytes_accessed=1 << 20, transcendentals=0
        ),
        name="pick_cols",
    )(index[:, None, :], x_train)


def pair_kernel(p_ref, b_ref, *refs):
    p = p_ref[...].reshape(-1, 128)
    for at in range(0, b_ref.shape[2], 256):
        value = matern_of(dot(p, b_ref[0, :, at : at + 256]))
        if len(refs) == 3:
            same = refs[0][...] == refs[1][:, at : at + 256]
            value = value + jnp.where(same, NOISE_VAR, 0.0)
        refs[-1][:, at : at + 256] = value.astype(BF16)


def pair_block(points, place, others, other, point_ids=None, other_ids=None, block=512):
    groups, rows, cols = points.shape[0], points.shape[0] * 64, others.shape[2]
    specs = [
        pl.BlockSpec((groups, 64, 128), lambda i: (0, place, 0)),
        pl.BlockSpec((1, 128, block), lambda i: (other, 0, i)),
    ]
    operands = [points, others]
    if point_ids is not None:
        specs += [pl.BlockSpec((rows, 1), lambda i: (0, 0)), pl.BlockSpec((1, block), lambda i: (0, i))]
        operands += [point_ids, other_ids]
    return pl.pallas_call(
        pair_kernel,
        grid=(cols // block,),
        in_specs=specs,
        out_specs=pl.BlockSpec((rows, block), lambda i: (0, i)),
        out_shape=jax.ShapeDtypeStruct((rows, cols), BF16),
        compiler_params=pltpu.CompilerParams(vmem_limit_bytes=24 << 20),
        cost_estimate=pl.CostEstimate(
            flops=12 * rows * cols, bytes_accessed=2 * rows * cols, transcendentals=2 * rows * cols
        ),
        name="pair_block",
    )(*operands)


def part_sums(p, x_ref, a_ref, f_ref, w, factor):
    total = dot(scaled_cos(dot(p, f_ref[...]), factor).astype(BF16), w)
    for at in range(0, x_ref.shape[1], 256):
        values = matern_of(dot(p, x_ref[:, at : at + 256])).astype(BF16)
        total = total + dot(values, a_ref[:, at : at + 256], NT)
    return total


def part_kernel(p_ref, x_ref, a_ref, f_ref, w_ref, o_ref, *, factor):
    total = part_sums(p_ref[...].reshape(-1, 128), x_ref, a_ref, f_ref, w_ref[...], factor)
    first = pl.program_id(0) == 0

    @pl.when(first)
    def _():
        o_ref[...] = total

    @pl.when(jnp.logical_not(first))
    def _():
        o_ref[...] += total


def part_block(points, place, x_wide, dual, f_wide, weights, factor, blocks=4):
    groups, rows, train = points.shape[0], points.shape[0] * 64, x_wide.shape[1]
    feats, paths = weights.shape
    return pl.pallas_call(
        lambda *refs: part_kernel(*refs, factor=factor),
        grid=(blocks,),
        in_specs=[
            pl.BlockSpec((groups, 64, 128), lambda i: (0, place, 0)),
            pl.BlockSpec((128, train // blocks), lambda i: (0, i)),
            pl.BlockSpec((paths, train // blocks), lambda i: (0, i)),
            pl.BlockSpec((128, feats // blocks), lambda i: (0, i)),
            pl.BlockSpec((feats // blocks, paths), lambda i: (i, 0)),
        ],
        out_specs=pl.BlockSpec((rows, paths), lambda i: (0, 0)),
        out_shape=jax.ShapeDtypeStruct((rows, paths), F32),
        compiler_params=pltpu.CompilerParams(vmem_limit_bytes=28 << 20),
        cost_estimate=pl.CostEstimate(
            flops=12 * rows * train, bytes_accessed=4 << 20, transcendentals=2 * rows * train
        ),
        name="part_block",
    )(points, x_wide, dual, f_wide, weights)


def first_kernel(p_ref, x_ref, a_ref, f_ref, w_ref, c_ref, o_ref, sum_ref, *, factor):
    col, row = pl.program_id(0), pl.program_id(1)
    weights = dot(w_ref[...], c_ref[...], NT).astype(BF16)
    total = part_sums(p_ref[...].reshape(-1, 128), x_ref, a_ref, f_ref, weights, factor)
    rows = total.shape[0]
    at = pl.ds(pl.multiple_of(row * rows, rows), rows)

    @pl.when(col == 0)
    def _():
        sum_ref[at, :] = total

    @pl.when(col > 0)
    def _():
        sum_ref[at, :] += total

    @pl.when(col == pl.num_programs(0) - 1)
    def _():
        done = sum_ref[at, :].astype(BF16).reshape(rows // 256, 2, 128, 64)
        for group in range(rows // 256):
            o_ref[group, :, :64] = done[group, 0]
            o_ref[group, :, 64:] = done[group, 1]


def first_block(points, x_wide, dual, f_wide, weights, chooser, factor, blocks=4):
    groups, train = points.shape[0], x_wide.shape[1]
    feats, paths = weights.shape
    some, chunk = dual.shape[0], 2
    return pl.pallas_call(
        lambda *refs: first_kernel(*refs, factor=factor),
        grid=(blocks, groups // chunk),
        in_specs=[
            pl.BlockSpec((chunk, 256, 128), lambda i, j: (j, 0, 0)),
            pl.BlockSpec((128, train // blocks), lambda i, j: (0, i)),
            pl.BlockSpec((some, train // blocks), lambda i, j: (0, i)),
            pl.BlockSpec((128, feats // blocks), lambda i, j: (0, i)),
            pl.BlockSpec((feats // blocks, paths), lambda i, j: (i, 0)),
            pl.BlockSpec((some, paths), lambda i, j: (0, 0)),
        ],
        out_specs=pl.BlockSpec((chunk, 128, 128), lambda i, j: (j, 0, 0)),
        out_shape=jax.ShapeDtypeStruct((groups, 128, 128), BF16),
        scratch_shapes=[pltpu.VMEM((groups * 256, some), F32)],
        compiler_params=pltpu.CompilerParams(vmem_limit_bytes=28 << 20),
        cost_estimate=pl.CostEstimate(
            flops=12 * groups * 256 * train, bytes_accessed=4 << 20, transcendentals=2 * groups * 256 * train
        ),
        name="first_block",
    )(points, x_wide, dual, f_wide, weights, chooser)


def merge_kernel(b_ref, o_ref):
    lane = lax.broadcasted_iota(jnp.int32, (128, 256), 0)
    path = lax.broadcasted_iota(jnp.int32, (128, 256), 1)
    inner = lane & 63
    core, x, own = inner >> 5, (inner >> 3) & 3, inner & 7
    for half in range(2):
        total = jnp.zeros((128, 256), F32)
        for z in range(4):
            to = ((x * 4 + z) * 2 + core) * 8 + own
            move = jnp.where((path == to) & (lane >> 6 == half), 1.0, 0.0).astype(BF16)
            total = total + dot(b_ref[z], move)
        o_ref[half * 128 : (half + 1) * 128, :] = total.astype(BF16)


def merge(blocks):
    return pl.pallas_call(
        merge_kernel, out_shape=jax.ShapeDtypeStruct((256, 256), BF16), name="merge"
    )(blocks)


def window_kernel(f_ref, w_ref, x_ref, o_ref, *, factor):
    cols = x_ref.shape[1]
    row = lax.broadcasted_iota(jnp.int32, (16, cols), 0)
    ones = jnp.where((row >= 3) & (row < 6), 1.0, 0.0).astype(BF16)
    x = jnp.concatenate([x_ref[...], ones, jnp.zeros((48, cols), BF16)], axis=0)
    for at in range(0, cols, 256):
        phi = scaled_cos(dot(f_ref[...], x[:, at : at + 256]), factor).astype(BF16)
        o_ref[:, at : at + 256] = dot(w_ref[...], phi)


def window_prior(f_rows, weights, x_window, factor, block=512):
    feats, paths, window = f_rows.shape[0], weights.shape[1], x_window.shape[1]
    return pl.pallas_call(
        lambda *refs: window_kernel(*refs, factor=factor),
        grid=(window // block,),
        in_specs=[
            pl.BlockSpec((feats, 128), lambda i: (0, 0)),
            pl.BlockSpec((paths, feats), lambda i: (0, 0)),
            pl.BlockSpec((x_window.shape[0], block), lambda i: (0, i)),
        ],
        out_specs=pl.BlockSpec((paths, block), lambda i: (0, i)),
        out_shape=jax.ShapeDtypeStruct((paths, window), F32),
        compiler_params=pltpu.CompilerParams(vmem_limit_bytes=24 << 20),
        cost_estimate=pl.CostEstimate(
            flops=24 * feats * window, bytes_accessed=4 * paths * window, transcendentals=feats * window
        ),
        name="window_prior",
    )(f_rows, weights.T, x_window)


def spread(index, rows, train):
    high, low = index >> 7, index & 127
    low_hot = (lax.broadcasted_iota(jnp.int32, (128, index.shape[1]), 0) == low).astype(F32).astype(BF16)
    tiles = [jnp.where(high == h, rows, 0.0) for h in range(train // 128)]
    return dot(jnp.concatenate(tiles, axis=0).astype(BF16), low_hot, NT)


def known_kernel(i_ref, t_ref, n_ref, a_ref, v_ref, cnt_ref, a1_ref, a2_ref):
    train = a_ref.shape[1]
    ones = jnp.ones((8, i_ref.shape[1]), F32)
    for t in range(STEPS):
        tiles = spread(i_ref[t : t + 1, :], ones, train)
        for h in range(train // 128):
            cnt_ref[t, :, h * 128 : (h + 1) * 128] = tiles[h * 8 : (h + 1) * 8, :]
    dual, velocity = a_ref[...], v_ref[...]
    fixed = n_ref[...] - t_ref[...]
    for t, out in enumerate((a1_ref, a2_ref)):
        gradient = cnt_ref[t] * (NOISE_VAR * dual + fixed)
        velocity = MOMENTUM * velocity - STEP_SIZE * gradient
        dual = dual + velocity
        out[...] = dual.astype(BF16)


def known_parts(index, targets, noise, dual, velocity):
    shape = dual.shape
    return pl.pallas_call(
        known_kernel,
        out_shape=(
            jax.ShapeDtypeStruct((STEPS,) + shape, F32),
            jax.ShapeDtypeStruct(shape, BF16),
            jax.ShapeDtypeStruct(shape, BF16),
        ),
        compiler_params=pltpu.CompilerParams(vmem_limit_bytes=32 << 20),
        cost_estimate=pl.CostEstimate(flops=1 << 23, bytes_accessed=1 << 20, transcendentals=0),
        name="known_parts",
    )(index, targets[None, :], noise, dual, velocity)


def place_kernel(i_ref, r_ref, o_ref):
    train = o_ref.shape[1]
    tiles = spread(i_ref[...], r_ref[...].astype(F32), train)
    for h in range(train // 128):
        o_ref[:, h * 128 : (h + 1) * 128] = tiles[h * 8 : (h + 1) * 8, :]


def place(index, rows, train):
    return pl.pallas_call(
        place_kernel,
        out_shape=jax.ShapeDtypeStruct((8, train), F32),
        compiler_params=pltpu.CompilerParams(vmem_limit_bytes=32 << 20),
        cost_estimate=pl.CostEstimate(flops=1 << 21, bytes_accessed=1 << 18, transcendentals=0),
        name="place",
    )(index[None, :], rows)


def finish_kernel(i_ref, r_ref, z0_ref, z1_ref, cnt_ref, t_ref, n_ref, a_ref, v_ref, ao_ref, vo_ref):
    train = a_ref.shape[1]
    rows = r_ref[...]
    coarse = rows.astype(BF16).astype(F32)
    tiles = spread(i_ref[...], coarse, train) + spread(i_ref[...], rows - coarse, train)
    dual, velocity = a_ref[...], v_ref[...]
    fixed = n_ref[...] - t_ref[...]
    z0 = z0_ref[...]
    velocity = MOMENTUM * velocity - STEP_SIZE * (z0 + cnt_ref[0] * (NOISE_VAR * dual + fixed))
    first = dual - STEP_SIZE * z0
    known = dual
    dual = dual + velocity
    change = -STEP_SIZE * z0
    gradient = z1_ref[...] + cnt_ref[1] * (NOISE_VAR * (dual - change) + fixed)
    velocity = MOMENTUM * velocity - STEP_SIZE * gradient
    dual = dual + velocity
    base = cnt_ref[2] * (NOISE_VAR * dual + fixed)
    for h in range(train // 128):
        at = slice(h * 128, (h + 1) * 128)
        vo_ref[:, at] = MOMENTUM * velocity[:, at] - STEP_SIZE * (
            base[:, at] + tiles[h * 8 : (h + 1) * 8, :]
        )
    ao_ref[...] = dual + vo_ref[...]


def finish(index, rows, z0, z1, counts, targets, noise, dual, velocity):
    shape = jax.ShapeDtypeStruct(dual.shape, F32)
    return pl.pallas_call(
        finish_kernel,
        out_shape=(shape, shape),
        compiler_params=pltpu.CompilerParams(vmem_limit_bytes=48 << 20),
        cost_estimate=pl.CostEstimate(flops=1 << 22, bytes_accessed=1 << 20, transcendentals=0),
        name="finish",
    )(index[None, :], rows, z0, z1, counts, targets[None, :], noise, dual, velocity)


def row_id_of(x, z, core):
    return (x * 4 + z) * 2 + core


X_GROUPS = [[row_id_of(x, z, c) for x in range(4)] for z in range(4) for c in range(2)]
Z_GROUPS = [[row_id_of(x, z, c) for z in range(4)] for x in range(4) for c in range(2)]
CORE_SWAP = [(i, i ^ 1) for i in range(32)]


def gather_groups(x, groups):
    spread_out = jnp.broadcast_to(x[None], (len(groups[0]),) + x.shape)
    return lax.all_to_all(spread_out, "row", 0, 0, axis_index_groups=groups, tiled=True)


def gather_core(x, row_id):
    other = lax.ppermute(x, "row", CORE_SWAP)
    even = row_id % 2 == 0
    return jnp.concatenate([jnp.where(even, x, other), jnp.where(even, other, x)], axis=0)


def after(*values):
    return lax.optimization_barrier(values)


def shards(
    x_train,
    targets,
    noise_draws,
    alpha_init,
    velocity_init,
    frequencies,
    phases,
    path_weights,
    x_window,
    batch_index,
):
    rows, cols = lax.axis_size("row"), lax.axis_size("col")
    row_id, col_id = lax.axis_index("row"), lax.axis_index("col")
    train = x_train.shape[1]
    batch_rows = batch_index.shape[1] // rows
    own_rows = batch_rows // cols
    group_rows = rows * own_rows
    paths = path_weights.shape[1]
    own_paths = paths // rows
    factor = (2.0 / (frequencies.shape[1] * cols)) ** 0.5
    dual, velocity, noise = alpha_init.T, velocity_init.T, noise_draws.T
    x_id, z_id, core_id = row_id // 8, row_id // 2 % 4, row_id % 2

    by_group = batch_index.reshape(STEPS, rows, cols, own_rows)
    mine = lax.dynamic_slice_in_dim(by_group, col_id, 1, 2)[:, :, 0] - col_id * train
    group_index = mine.reshape(STEPS, group_rows)
    by_place = mine.reshape(STEPS, 4, 4, 2, own_rows)
    sorted_index = by_place[:2].transpose(0, 3, 1, 2, 4).reshape(2, group_rows)
    near = lax.dynamic_slice(by_place[0], (x_id, 0, core_id, 0), (1, 4, 1, own_rows)).reshape(-1)
    own_index = lax.dynamic_slice_in_dim(mine[1:], row_id, 1, 1).reshape(-1)
    own_index = jnp.concatenate([near, own_index])

    gathered0 = gather_groups(dual.astype(BF16), X_GROUPS)
    own_points, x_wide, f_wide = setup(own_index, x_train, frequencies, phases)
    counts, known1, known2 = known_parts(group_index, targets, noise, dual, velocity)
    gathered0, own_points, counts, known1, known2 = after(gathered0, own_points, counts, known1, known2)
    gathered1 = lax.all_gather(known1, "row", axis=0, tiled=True)
    gathered2 = lax.all_gather(known2, "row", axis=0, tiled=True)
    points = lax.all_to_all(
        jnp.broadcast_to(own_points[None], (cols,) + own_points.shape), "col", 0, 0, tiled=True
    )
    gathered0 = gather_core(gathered0, row_id).reshape(paths // 4, train)
    window_part = window_prior(f_wide.T, path_weights, x_window, factor)
    points, window_part, gathered0 = after(points, window_part, gathered0)
    prior_window = lax.psum_scatter(window_part, "col", scatter_dimension=0, tiled=True)

    here = lax.broadcasted_iota(jnp.int32, (paths // 4, paths), 0)
    here = (((here >> 3) % 4 * 4 + z_id) * 2 + (here >> 5)) * own_paths + here % own_paths
    here = (lax.broadcasted_iota(jnp.int32, (paths // 4, paths), 1) == here).astype(BF16)
    blocks = first_block(points, x_wide, gathered0, f_wide, path_weights, here, factor)
    row_index = lax.dynamic_slice_in_dim(batch_index[1], row_id * batch_rows, batch_rows, 0) - col_id * train

    def send_cols(part):
        return lax.all_to_all(part.astype(BF16).reshape(cols, own_rows, paths), "col", 0, 0, tiled=True)

    def add_up(blocks):
        return jnp.sum(blocks.astype(F32), axis=0)

    chooser = lax.broadcasted_iota(jnp.int32, (own_paths, paths), 1)
    chooser = chooser - own_paths * row_id == lax.broadcasted_iota(jnp.int32, (own_paths, paths), 0)
    chooser = chooser.astype(BF16)

    blocks = lax.all_to_all(blocks, "col", 0, 0, tiled=True)
    group_points = pick_cols(sorted_index, x_train)
    blocks, group_points = after(blocks, group_points)
    terms0 = gather_groups(add_up(blocks).astype(BF16), Z_GROUPS)
    between10 = pair_block(points, 4, group_points, 0, row_index[:, None], sorted_index[:1])
    between20 = pair_block(points, 5, group_points, 0)
    terms0, between10, between20 = after(terms0, between10, between20)
    terms0 = gather_groups(merge(terms0), X_GROUPS)
    part1 = part_block(points, 4, x_wide, gathered1, f_wide, path_weights, factor)
    terms0, part1 = after(terms0, part1)
    terms0 = gather_core(terms0, row_id).reshape(group_rows, paths)

    blocks = send_cols(part1 - STEP_SIZE * dot(between10, terms0))
    between21 = pair_block(points, 5, group_points, 1)
    blocks, between21 = after(blocks, between21)
    terms1 = gather_groups(add_up(blocks).astype(BF16), Z_GROUPS)
    part2 = part_block(points, 5, x_wide, gathered2, f_wide, path_weights, factor)
    terms1, part2 = after(terms1, part2)
    terms1 = gather_groups(terms1, X_GROUPS)
    part2 = part2 - (STEP_SIZE * (1.0 + MOMENTUM)) * dot(between20, terms0)
    terms1, part2 = after(terms1, part2)
    terms1 = gather_core(terms1, row_id).reshape(group_rows, paths)

    blocks = send_cols(part2 - STEP_SIZE * dot(between21, terms1))
    z0 = place(sorted_index[0], dot(chooser, terms0, NT), train)
    blocks, z0 = after(blocks, z0)
    blocks = lax.all_to_all(add_up(blocks).T.reshape(rows, own_paths, own_rows), "row", 0, 0, tiled=True)
    z1 = place(sorted_index[1], dot(chooser, terms1, NT), train)
    blocks, z1 = after(blocks, z1)
    own_terms = blocks.transpose(1, 0, 2).reshape(own_paths, group_rows)
    dual, velocity = finish(
        group_index[2], own_terms, z0, z1, counts, targets, noise, dual, velocity
    )
    return (dual.T, velocity.T, prior_window)


def solution(mesh):
    placed = (
        P(None, "col"),
        P("col"),
        P("col", "row"),
        P("col", "row"),
        P("col", "row"),
        P(None, "col"),
        P("col"),
        P("col", None),
        P(None, "row"),
        P(),
    )
    return jax.shard_map(
        shards,
        mesh=mesh,
        in_specs=placed,
        out_specs=(P("col", "row"), P("col", "row"), P("col", "row")),
        check_vma=False,
    )
```

time: 249 us -> 221 us (0.89)
  blocking collectives: 64.3 us -> 0 us
  starting transfers between devices: 36.9 us -> 61.4 us
  waiting for transfers between devices: 35.1 us -> 43.7 us
  Pallas kernels: 47.3 us -> 54.9 us
  matrix products: 14.7 us -> 7.39 us
    all_to_all x5 -> x0, blocking collectives: 64.3 us -> none  [the longest x3 41.8 us: gather_groups(): lax.all_to_all(spread_out, 'row', 0, 0, axis_index_groups=groups, tiled=T...]
    all_to_all x3 -> x5, starting transfers between devices: 12.7 us -> 28.2 us  [gather_groups(): lax.all_to_all(spread_out, 'row', 0, 0, axis_index_groups=groups, tiled=T...]
    pallas_call x9, Pallas kernels: 35.8 us -> 46.6 us  [the longest x1 21.9 us: first_block(): pl.pallas_call(lambda *refs: first_kernel(*refs, factor=factor), grid=(bl...]
    all_to_all x2 -> x4, starting transfers between devices: 9.38 us -> 19.7 us  [the longest x2 9.08 us: send_cols(): lax.all_to_all(part.astype(BF16).reshape(cols, own_rows, paths), 'col', 0...]
    dot_general x8 -> x5, matrix products: 14.7 us -> 7.39 us  [dot(): return lax.dot_general(a, b, dims, preferred_element_type=F32)]
    another operation x7 -> x0, other arithmetic: 6.37 us -> none  [the longest x6 5.6 us: gather_rows(): jnp.stack([jnp.where(even, x, other), jnp.where(even, other, x)], axis=2)]
    all_to_all x2 -> x4, waiting for transfers between devices: 13.7 us -> 18.7 us  [the longest x2 11 us: send_cols(): lax.all_to_all(part.astype(BF16).reshape(cols, own_rows, paths), 'col', 0...]
    all_to_all x1, waiting for transfers between devices: 9.15 us -> 13.4 us  [shards(): lax.all_to_all(jnp.broadcast_to(own_points[None], (cols,) + own_points.sh...]
  transfers between devices with their start and end apart: 12 -> 16, of which waited for: 4 -> 9; matrix products, arithmetic and copies ran while one was open for 13% -> 13% of each run, Pallas kernels for 18% -> 25%
where the time goes in v2:
time: 221 us; the launch traced here: 219 us
  starting transfers between devices  61.4 us (28%)
  Pallas kernels  54.9 us (25%)
  waiting for transfers between devices  43.7 us (20%)
  local copies, waits for them, and re-layouts  27 us (12%)
  between operations  16.1 us (7%)
  other arithmetic  8.64 us (4%)
  matrix products  7.39 us (3%)
    all_to_all x5, starting transfers between devices, gather_groups(): lax.all_to_all(spread_out, 'row', 0, 0, axis_index_groups=groups, tiled=T...  28.2 us
    pallas_call x1, Pallas kernels, first_block(): pl.pallas_call(lambda *refs: first_kernel(*refs, factor=factor), grid=(bl...  21.9 us
    unnamed x64, local copies, waits for them, and re-layouts  14.6 us
    all_to_all x1, waiting for transfers between devices, shards(): lax.all_to_all(jnp.broadcast_to(own_points[None], (cols,) + own_points.sh...  13.4 us
    all_to_all x2, waiting for transfers between devices, send_cols(): lax.all_to_all(part.astype(BF16).reshape(cols, own_rows, paths), 'col', 0...  11 us
    pallas_call x2, Pallas kernels, part_block(): pl.pallas_call(lambda *refs: part_kernel(*refs, factor=factor), grid=(blo...  9.93 us
    ppermute x3, starting transfers between devices, gather_core(): other = lax.ppermute(x, 'row', CORE_SWAP)  9.32 us
    all_to_all x2, starting transfers between devices, send_cols(): lax.all_to_all(part.astype(BF16).reshape(cols, own_rows, paths), 'col', 0...  9.08 us
  transfers between devices with their start and end apart: 16, of which 9 were waited for; matrix products, arithmetic and copies ran while one was open for 13% of the time, Pallas kernels for 25%

profile of v2, /device:TPU:1, one launch (start us, length us, event | category | flops | bytes accessed | tf_op | source)
XLA Modules:
  0.0 219.2 jit_solution(2534430464191835084)
XLA Ops:
  8.1 1.0 bitcast_convert_fusion
  9.1 0.7 broadcast_in_dim.18
  9.8 5.0 %all-to-all-start = ((bf16[4,8,4096]{2,1,0:T(8,128)(2,1)}), bf16[4,8,4096]{2,1,0:T(8,128)(2,1)}, u32[]{:S(2)}, u32[]{:S(2)}) async-start(bf16[4,8,4096]{2,1,0:T(8,128)(2,1)} %broadcast_in_dim.18), calls=%async_computation | async-start | bytes 524288 | tf_op jit(solution)/shard_map/all_to_all | solution.py:420
  14.8 1.2 reshape.78
  17.2 1.4 setup.1
  18.7 1.9 known_parts.1
  20.7 0.7 all-gather.5.cloned.1.call-update
  23.1 3.4 %collective-permute-start = (bf16[4,8,4096]{2,1,0:T(8,128)(2,1)}, bf16[4,8,4096]{2,1,0:T(8,128)(2,1)}, u32[]{:S(2)}, u32[]{:S(2)}) collective-permute-start(bf16[4,8,4096]{2,1,0:T(8,128)(2,1)} %all-to-all-done), channel_id=1, source_target_pairs={{0,8},{8,0},{16,24},{24,16},{32,40},{40,32},{48,56},{56,48},{64,72... | collective-permute-start | bytes 786440 | tf_op jit(solution)/shard_map/ppermute | solution.py:424
  27.2 4.6 %window_prior.1 = f32[256,2048]{1,0:T(8,128)} custom-call(bf16[512,128]{1,0:T(8,128)(2,1)S(1)} %bitcast.47, bf16[256,512]{1,0:T(8,128)(2,1)S(1)} %bitcast.42, bf16[64,2048]{1,0:T(8,128)(2,1)S(1)} %copy-done.8), custom_call_target="tpu_custom_call" | custom-call | flops 25165824 | bytes 2097152 | tf_op jit(solution)/shard_map/window_prior/pallas_call | solution.py:300
  31.9 0.8 fusion.5.refs_5_
  32.7 1.0 broadcast_in_dim.22
  33.7 4.1 %all-to-all-start.1 = ((bf16[8,384,128]{2,1,0:T(8,128)(2,1)}), bf16[8,384,128]{2,1,0:T(8,128)(2,1)S(1)}, u32[]{:S(2)}, u32[]{:S(2)}) async-start(bf16[8,384,128]{2,1,0:T(8,128)(2,1)} %broadcast_in_dim.22), calls=%async_computation.1 | async-start | bytes 1572864 | tf_op jit(solution)/shard_map/all_to_all | solution.py:472
  37.8 1.1 broadcast_select_fusion.5
  38.9 13.4 %all-to-all-done.1.refs_0_.p_ref = bf16[8,384,128]{2,1,0:T(8,128)(2,1)S(1)} async-done(((bf16[8,384,128]{2,1,0:T(8,128)(2,1)}), bf16[8,384,128]{2,1,0:T(8,128)(2,1)S(1)}, u32[]{:S(2)}, u32[]{:S(2)}) %all-to-all-start.1) | async-done | bytes 786464 | tf_op jit(solution)/shard_map/all_to_all | solution.py:472
  52.3 1.2 copy-done.16
  53.5 21.9 %first_block.1 = bf16[8,128,128]{2,1,0:T(8,128)(2,1)} custom-call(bf16[8,384,128]{2,1,0:T(8,128)(2,1)S(1)} %all-to-all-done.1.refs_0_.p_ref, bf16[128,4096]{1,0:T(8,128)(2,1)S(1)} %copy-done.16, bf16[64,4096]{1,0:T(8,128)(2,1)S(1)} %maximum_bitcast_fusion.refs_2_, bf16[128,512]{1,0:T(8,128)(2,1)S(1)} %get-tuple-element.41.refs_3_, ...), custom_call_target="tpu_custom_call" | custom-call | flops 100663296 | bytes 4194304 | tf_op jit(solution)/shard_map/first_block/pallas_call | solution.py:246
  75.4 4.1 %all-to-all-start.2 = ((bf16[8,128,128]{2,1,0:T(8,128)(2,1)}), bf16[8,128,128]{2,1,0:T(8,128)(2,1)}, u32[]{:S(2)}, u32[]{:S(2)}) async-start(bf16[8,128,128]{2,1,0:T(8,128)(2,1)} %first_block.1), calls=%async_computation.2 | async-start | bytes 524288 | tf_op jit(solution)/shard_map/all_to_all | solution.py:496
  79.5 1.0 slice.45
  81.3 0.7 broadcast_in_dim_reshape.3.i_ref
  82.1 0.7 copy-done.10
  82.8 3.8 %pick_cols.1.b_ref = bf16[2,128,2048]{2,1,0:T(8,128)(2,1)S(1)} custom-call(s32[2,1,2048]{2,1,0:T(1,128)S(1)} %copy-done.10, bf16[64,4096]{1,0:T(8,128)(2,1)S(1)} %copy-done), custom_call_target="tpu_custom_call" | custom-call | flops 62914560 | bytes 1048576 | tf_op jit(solution)/shard_map/pick_cols/pallas_call | solution.py:124
  86.6 1.0 reduce_sum.33
  88.3 6.9 %all-to-all-start.3 = ((bf16[4,128,128]{2,1,0:T(8,128)(2,1)}), bf16[4,128,128]{2,1,0:T(8,128)(2,1)S(1)}, u32[]{:S(2)}, u32[]{:S(2)}) async-start(bf16[4,128,128]{2,1,0:T(8,128)(2,1)} %broadcast_in_dim.23), calls=%async_computation.3 | async-start | bytes 262144 | tf_op jit(solution)/shard_map/all_to_all | solution.py:420
  95.2 1.3 fusion.13
  96.6 2.2 pair_block.4
  98.8 1.4 copy-done.19
  100.2 2.5 %pair_block.3 = bf16[512,2048]{1,0:T(8,128)(2,1)S(1)} custom-call(bf16[8,384,128]{2,1,0:T(8,128)(2,1)S(1)} %all-to-all-done.1.refs_0_.p_ref, bf16[2,128,2048]{2,1,0:T(8,128)(2,1)S(1)} %pick_cols.1.b_ref, s32[512,1]{1,0:T(8,128)S(1)} %copy.32.refs_0_, s32[1,2048]{1,0:T(1,128)S(1)} %slice.47.refs_1_.i_ref), custom_call_target="tpu_custom_call" | custom-call | flops 12582912 | bytes 2097152 | tf_op jit(solution)/shard_map/pair_block/pallas_call | solution.py:161
  102.7 1.3 copy-done.1
  104.7 1.9 merge.1
  106.5 1.8 broadcast_in_dim.24
  108.3 4.2 %all-to-all-start.4 = ((bf16[4,256,256]{2,1,0:T(8,128)(2,1)}), bf16[4,256,256]{2,1,0:T(8,128)(2,1)}, u32[]{:S(2)}, u32[]{:S(2)}) async-start(bf16[4,256,256]{2,1,0:T(8,128)(2,1)} %broadcast_in_dim.24), calls=%async_computation.4 | async-start | bytes 1048576 | tf_op jit(solution)/shard_map/all_to_all | solution.py:420
  112.6 1.6 copy-done.14
  114.2 1.2 copy-done.17
  115.4 5.0 %part_block.2 = f32[512,256]{1,0:T(8,128)S(1)} custom-call(bf16[8,384,128]{2,1,0:T(8,128)(2,1)S(1)} %all-to-all-done.1.refs_0_.p_ref, bf16[128,4096]{1,0:T(8,128)(2,1)S(1)} %copy-done.17, bf16[256,4096]{1,0:T(8,128)(2,1)S(1)} %copy-done.14, bf16[128,512]{1,0:T(8,128)(2,1)S(1)} %get-tuple-element.41.refs_3_, bf16[512,256]{1,0:T(8,128)(2,1)S(1)} %copy-done.7), custom_call_target="tpu_custom_call" | custom-call | flops 25165824 | bytes 4194304 | tf_op jit(solution)/shard_map/part_block/pallas_call | solution.py:199
  120.4 0.8 copy-done.22
  121.2 1.0 all-to-all-done.4
  122.1 2.3 %collective-permute-start.1 = (bf16[4,256,256]{2,1,0:T(8,128)(2,1)}, bf16[4,256,256]{2,1,0:T(8,128)(2,1)}, u32[]{:S(2)}, u32[]{:S(2)}) collective-permute-start(bf16[4,256,256]{2,1,0:T(8,128)(2,1)} %all-to-all-done.4), channel_id=1, source_target_pairs={{0,8},{8,0},{16,24},{24,16},{32,40},{40,32},{48,56},{56,48},{64,72... | collective-permute-start | bytes 1572872 | tf_op jit(solution)/shard_map/ppermute | solution.py:424
  124.5 1.8 collective-permute-done.1
  126.3 1.3 broadcast_select_fusion.3
  127.7 1.4 fusion.3
  129.2 5.7 %all-to-all-start.5 = ((bf16[8,64,256]{2,1,0:T(8,128)(2,1)}), bf16[8,64,256]{2,1,0:T(8,128)(2,1)S(1)}, u32[]{:S(2)}, u32[]{:S(2)}) async-start(bf16[8,64,256]{2,1,0:T(8,128)(2,1)} %bitcast.61), calls=%async_computation.5 | async-start | bytes 524288 | tf_op jit(solution)/shard_map/all_to_all | solution.py:487
  134.8 2.2 pair_block.5
  137.0 1.3 copy-done.20
  138.4 5.1 %all-to-all-done.5 = bf16[8,64,256]{2,1,0:T(8,128)(2,1)S(1)} async-done(((bf16[8,64,256]{2,1,0:T(8,128)(2,1)}), bf16[8,64,256]{2,1,0:T(8,128)(2,1)S(1)}, u32[]{:S(2)}, u32[]{:S(2)}) %all-to-all-start.5) | async-done | bytes 262176 | tf_op jit(solution)/shard_map/all_to_all | solution.py:487
  144.2 8.7 %all-to-all-start.6 = ((bf16[4,64,256]{2,1,0:T(8,128)(2,1)}), bf16[4,64,256]{2,1,0:T(8,128)(2,1)S(1)}, u32[]{:S(2)}, u32[]{:S(2)}) async-start(bf16[4,64,256]{2,1,0:T(8,128)(2,1)} %broadcast_in_dim.25), calls=%async_computation.6 | async-start | bytes 262144 | tf_op jit(solution)/shard_map/all_to_all | solution.py:420
  152.9 1.6 copy-done.13
  154.5 1.2 copy-done.18
  155.7 5.0 %part_block.3 = f32[512,256]{1,0:T(8,128)S(1)} custom-call(bf16[8,384,128]{2,1,0:T(8,128)(2,1)S(1)} %all-to-all-done.1.refs_0_.p_ref, bf16[128,4096]{1,0:T(8,128)(2,1)S(1)} %copy-done.18, bf16[256,4096]{1,0:T(8,128)(2,1)S(1)} %copy-done.13, bf16[128,512]{1,0:T(8,128)(2,1)S(1)} %get-tuple-element.41.refs_3_, bf16[512,256]{1,0:T(8,128)(2,1)S(1)} %copy-done.7), custom_call_target="tpu_custom_call" | custom-call | flops 25165824 | bytes 4194304 | tf_op jit(solution)/shard_map/part_block/pallas_call | solution.py:199
  160.7 1.8 all-to-all-done.6
  162.5 0.9 broadcast_in_dim.26
  163.3 3.5 %all-to-all-start.7 = ((bf16[4,4,64,256]{3,2,1,0:T(8,128)(2,1)}), bf16[4,4,64,256]{3,2,1,0:T(8,128)(2,1)S(1)}, u32[]{:S(2)}, u32[]{:S(2)}) async-start(bf16[4,4,64,256]{3,2,1,0:T(8,128)(2,1)} %broadcast_in_dim.26), calls=%async_computation.7 | async-start | bytes 1048576 | tf_op jit(solution)/shard_map/all_to_all | solution.py:420
  166.8 2.6 %fusion.1 = f32[512,256]{1,0:T(8,128)S(1)} fusion(f32[512,256]{1,0:T(8,128)S(1)} %part_block.3, bf16[512,2048]{1,0:T(8,128)(2,1)} %copy-done.19, bf16[2048,256]{1,0:T(8,128)(2,1)} %bitcast.52), kind=kOutput, calls=%fused_computation.3 | convolution fusion | flops 537133056 | bytes 4194304 | tf_op jit(solution)/shard_map/dot_general | solution.py:31
  169.4 4.7 %all-to-all-done.7 = bf16[4,4,64,256]{3,2,1,0:T(8,128)(2,1)S(1)} async-done(((bf16[4,4,64,256]{3,2,1,0:T(8,128)(2,1)}), bf16[4,4,64,256]{3,2,1,0:T(8,128)(2,1)S(1)}, u32[]{:S(2)}, u32[]{:S(2)}) %all-to-all-start.7) | async-done | bytes 524320 | tf_op jit(solution)/shard_map/all_to_all | solution.py:420
  174.1 3.7 %collective-permute-start.2 = (bf16[4,4,64,256]{3,2,1,0:T(8,128)(2,1)S(1)}, bf16[4,4,64,256]{3,2,1,0:T(8,128)(2,1)S(1)}, u32[]{:S(2)}, u32[]{:S(2)}) collective-permute-start(bf16[4,4,64,256]{3,2,1,0:T(8,128)(2,1)S(1)} %all-to-all-done.7), channel_id=1, source_target_pairs={{0,8},{8,0},{16,24},{24,16},{32,40},{40,32},{48,56},{56,48},{64,72... | collective-permute-start | bytes 1572872 | tf_op jit(solution)/shard_map/ppermute | solution.py:424
  177.8 1.5 collective-permute-done.2
  179.5 1.4 fusion.4
  180.9 3.4 %all-to-all-start.8 = ((bf16[8,64,256]{2,1,0:T(8,128)(2,1)}), bf16[8,64,256]{2,1,0:T(8,128)(2,1)S(1)}, u32[]{:S(2)}, u32[]{:S(2)}) async-start(bf16[8,64,256]{2,1,0:T(8,128)(2,1)} %bitcast.15), calls=%async_computation.8 | async-start | bytes 524288 | tf_op jit(solution)/shard_map/all_to_all | solution.py:487
  185.4 5.9 %all-to-all-done.8 = bf16[8,64,256]{2,1,0:T(8,128)(2,1)S(1)} async-done(((bf16[8,64,256]{2,1,0:T(8,128)(2,1)}), bf16[8,64,256]{2,1,0:T(8,128)(2,1)S(1)}, u32[]{:S(2)}, u32[]{:S(2)}) %all-to-all-start.8) | async-done | bytes 262176 | tf_op jit(solution)/shard_map/all_to_all | solution.py:487
  191.5 0.8 reshape.100
  192.2 6.6 %all-to-all-start.9 = ((f32[32,1,512]{2,1,0:T(1,128)}), f32[32,1,512]{2,1,0:T(1,128)S(1)}, u32[]{:S(2)}, u32[]{:S(2)}) async-start(f32[32,1,512]{2,1,0:T(1,128)} %reshape.100), calls=%async_computation.9 | async-start | bytes 131072 | tf_op jit(solution)/shard_map/all_to_all | solution.py:522
  198.8 1.6 fusion.6.r_ref
  200.9 7.7 %all-to-all-done.9 = f32[32,1,512]{2,1,0:T(1,128)S(1)} async-done(((f32[32,1,512]{2,1,0:T(1,128)}), f32[32,1,512]{2,1,0:T(1,128)S(1)}, u32[]{:S(2)}, u32[]{:S(2)}) %all-to-all-start.9) | async-done | bytes 65568 | tf_op jit(solution)/shard_map/all_to_all | solution.py:522
  209.2 0.8 reduce.10
  210.2 1.6 finish.1
  (105 shorter events, 9.5 us)
Async XLA Ops:
  8.0 10.6 %copy-start.3 = (f32[4096,8]{0,1:T(8,128)S(1)}, f32[4096,8]{0,1:T(8,128)}, u32[]{:S(2)}) copy-start(f32[4096,8]{0,1:T(8,128)} %param.13) | copy-start | bytes 393220
  8.0 9.2 %copy-start = (bf16[64,4096]{1,0:T(8,128)(2,1)S(1)}, bf16[64,4096]{1,0:T(8,128)(2,1)}, u32[]{:S(2)}) copy-start(bf16[64,4096]{1,0:T(8,128)(2,1)} %x_ref.3) | copy-start | bytes 1572868
  8.0 9.2 %copy-start.12 = (f32[512]{0:T(512)S(1)}, f32[512]{0:T(512)}, u32[]{:S(2)}) copy-start(f32[512]{0:T(512)} %param.16) | copy-start | bytes 6148
  8.0 9.2 %copy-start.11 = (bf16[64,512]{1,0:T(8,128)(2,1)S(1)}, bf16[64,512]{1,0:T(8,128)(2,1)}, u32[]{:S(2)}) copy-start(bf16[64,512]{1,0:T(8,128)(2,1)} %f_ref.1) | copy-start | bytes 196612
  8.0 10.6 %copy-start.5 = (f32[4096,8]{0,1:T(8,128)S(1)}, f32[4096,8]{0,1:T(8,128)}, u32[]{:S(2)}) copy-start(f32[4096,8]{0,1:T(8,128)} %param.14) | copy-start | bytes 393220
  8.0 10.6 %copy-start.4 = (f32[4096,8]{0,1:T(8,128)S(1)}, f32[4096,8]{0,1:T(8,128)}, u32[]{:S(2)}) copy-start(f32[4096,8]{0,1:T(8,128)} %param.12) | copy-start | bytes 393220
  8.1 10.6 %copy-start.9 = (f32[4096]{0:T(1024)S(1)}, f32[4096]{0:T(1024)}, u32[]{:S(2)}) copy-start(f32[4096]{0:T(1024)} %param.11) | copy-start | bytes 49156
  8.1 18.9 %copy-start.6 = (bf16[512,256]{1,0:T(8,128)(2,1)S(1)}, bf16[512,256]{1,0:T(8,128)(2,1)}, u32[]{:S(2)}) copy-start(bf16[512,256]{1,0:T(8,128)(2,1)} %refs_4_.5) | copy-start | bytes 786436
  9.8 17.4 %copy-start.8 = (bf16[64,2048]{1,0:T(8,128)(2,1)S(1)}, bf16[64,2048]{1,0:T(8,128)(2,1)}, u32[]{:S(2)}) copy-start(bf16[64,2048]{1,0:T(8,128)(2,1)} %refs_2_.1) | copy-start | bytes 786436
  9.8 10.8 %all-to-all-start = ((bf16[4,8,4096]{2,1,0:T(8,128)(2,1)}), bf16[4,8,4096]{2,1,0:T(8,128)(2,1)}, u32[]{:S(2)}, u32[]{:S(2)}) async-start(bf16[4,8,4096]{2,1,0:T(8,128)(2,1)} %broadcast_in_dim.18), calls=%async_computation | async-start | bytes 524288 | tf_op jit(solution)/shard_map/all_to_all | solution.py:420
  14.8 97.8 %all-gather.3.cloned.1.call-start = ((), (), s32[]{:S(2)}) async-start(), calls=%async_computation.11 | async-start | bytes 2162688 | tf_op jit(solution)/shard_map/all_gather | solution.py:470
  18.6 13.2 %copy-start.15 = (bf16[128,4096]{1,0:T(8,128)(2,1)}, bf16[128,4096]{1,0:T(8,128)(2,1)S(1)}, u32[]{:S(2)}) copy-start(bf16[128,4096]{1,0:T(8,128)(2,1)S(1)} %get-tuple-element.44.refs_1_) | copy-start | bytes 3145732
  20.6 132.3 %all-gather.5.cloned.1.call-start = ((), (), s32[]{:S(2)}) async-start(), calls=%async_computation.12 | async-start | bytes 2162688 | tf_op jit(solution)/shard_map/all_gather | solution.py:471
  23.1 14.7 %collective-permute-start = (bf16[4,8,4096]{2,1,0:T(8,128)(2,1)}, bf16[4,8,4096]{2,1,0:T(8,128)(2,1)}, u32[]{:S(2)}, u32[]{:S(2)}) collective-permute-start(bf16[4,8,4096]{2,1,0:T(8,128)(2,1)} %all-to-all-done), channel_id=1, source_target_pairs={{0,8},{8,0},{16,24},{24,16},{32,40},{40,32},{48,56},{56,48},{64,72... | collective-permute-start | bytes 786440 | tf_op jit(solution)/shard_map/ppermute | solution.py:424
  33.7 18.6 %all-to-all-start.1 = ((bf16[8,384,128]{2,1,0:T(8,128)(2,1)}), bf16[8,384,128]{2,1,0:T(8,128)(2,1)S(1)}, u32[]{:S(2)}, u32[]{:S(2)}) async-start(bf16[8,384,128]{2,1,0:T(8,128)(2,1)} %broadcast_in_dim.22), calls=%async_computation.1 | async-start | bytes 1572864 | tf_op jit(solution)/shard_map/all_to_all | solution.py:472
  52.3 1.2 copy-start.16
  75.4 11.2 %all-to-all-start.2 = ((bf16[8,128,128]{2,1,0:T(8,128)(2,1)}), bf16[8,128,128]{2,1,0:T(8,128)(2,1)}, u32[]{:S(2)}, u32[]{:S(2)}) async-start(bf16[8,128,128]{2,1,0:T(8,128)(2,1)} %first_block.1), calls=%async_computation.2 | async-start | bytes 524288 | tf_op jit(solution)/shard_map/all_to_all | solution.py:496
  80.7 0.6 copy-start.28
  82.0 0.7 copy-start.10
  88.3 15.7 %all-to-all-start.3 = ((bf16[4,128,128]{2,1,0:T(8,128)(2,1)}), bf16[4,128,128]{2,1,0:T(8,128)(2,1)S(1)}, u32[]{:S(2)}, u32[]{:S(2)}) async-start(bf16[4,128,128]{2,1,0:T(8,128)(2,1)} %broadcast_in_dim.23), calls=%async_computation.3 | async-start | bytes 262144 | tf_op jit(solution)/shard_map/all_to_all | solution.py:420
  98.8 1.4 copy-start.19
  100.2 12.4 %copy-start.7 = (bf16[512,256]{1,0:T(8,128)(2,1)S(1)}, bf16[512,256]{1,0:T(8,128)(2,1)}, u32[]{:S(2)}) copy-start(bf16[512,256]{1,0:T(8,128)(2,1)} %refs_4_.5) | copy-start | bytes 786436
  102.7 1.3 copy-start.1
  104.0 0.7 copy-start.27
  108.3 13.8 %all-to-all-start.4 = ((bf16[4,256,256]{2,1,0:T(8,128)(2,1)}), bf16[4,256,256]{2,1,0:T(8,128)(2,1)}, u32[]{:S(2)}, u32[]{:S(2)}) async-start(bf16[4,256,256]{2,1,0:T(8,128)(2,1)} %broadcast_in_dim.24), calls=%async_computation.4 | async-start | bytes 1048576 | tf_op jit(solution)/shard_map/all_to_all | solution.py:420
  112.5 99.3 %reduce-scatter.2.cloned.1.call-start = ((), (), s32[]{:S(2)}) async-start(), calls=%async_computation.13 | async-start | bytes 2359296 | tf_op jit(solution)/shard_map/reduce_scatter | solution.py:478
  112.6 1.6 copy-start.14
  114.2 1.2 copy-start.17
  120.4 0.8 copy-start.22
  122.1 4.2 %collective-permute-start.1 = (bf16[4,256,256]{2,1,0:T(8,128)(2,1)}, bf16[4,256,256]{2,1,0:T(8,128)(2,1)}, u32[]{:S(2)}, u32[]{:S(2)}) collective-permute-start(bf16[4,256,256]{2,1,0:T(8,128)(2,1)} %all-to-all-done.4), channel_id=1, source_target_pairs={{0,8},{8,0},{16,24},{24,16},{32,40},{40,32},{48,56},{56,48},{64,72... | collective-permute-start | bytes 1572872 | tf_op jit(solution)/shard_map/ppermute | solution.py:424
  124.4 3.3 %copy-start.2 = (bf16[512,2048]{1,0:T(8,128)(2,1)S(1)}, bf16[512,2048]{1,0:T(8,128)(2,1)}, u32[]{:S(2)}) copy-start(bf16[512,2048]{1,0:T(8,128)(2,1)} %copy-done.1) | copy-start | bytes 6291460
  124.4 3.3 %copy-start.23 = (f32[512,256]{1,0:T(8,128)S(1)}, f32[512,256]{1,0:T(8,128)}, u32[]{:S(2)}) copy-start(f32[512,256]{1,0:T(8,128)} %copy-done.22) | copy-start | bytes 1572868
  127.7 1.5 copy-start.24
  129.2 14.3 %all-to-all-start.5 = ((bf16[8,64,256]{2,1,0:T(8,128)(2,1)}), bf16[8,64,256]{2,1,0:T(8,128)(2,1)S(1)}, u32[]{:S(2)}, u32[]{:S(2)}) async-start(bf16[8,64,256]{2,1,0:T(8,128)(2,1)} %bitcast.61), calls=%async_computation.5 | async-start | bytes 524288 | tf_op jit(solution)/shard_map/all_to_all | solution.py:487
  137.0 1.4 copy-start.20
  144.2 18.3 %all-to-all-start.6 = ((bf16[4,64,256]{2,1,0:T(8,128)(2,1)}), bf16[4,64,256]{2,1,0:T(8,128)(2,1)S(1)}, u32[]{:S(2)}, u32[]{:S(2)}) async-start(bf16[4,64,256]{2,1,0:T(8,128)(2,1)} %broadcast_in_dim.25), calls=%async_computation.6 | async-start | bytes 262144 | tf_op jit(solution)/shard_map/all_to_all | solution.py:420
  152.9 1.6 copy-start.13
  154.5 1.2 copy-start.18
  163.3 10.8 %all-to-all-start.7 = ((bf16[4,4,64,256]{3,2,1,0:T(8,128)(2,1)}), bf16[4,4,64,256]{3,2,1,0:T(8,128)(2,1)S(1)}, u32[]{:S(2)}, u32[]{:S(2)}) async-start(bf16[4,4,64,256]{3,2,1,0:T(8,128)(2,1)} %broadcast_in_dim.26), calls=%async_computation.7 | async-start | bytes 1048576 | tf_op jit(solution)/shard_map/all_to_all | solution.py:420
  174.1 5.4 %copy-start.21 = (bf16[512,2048]{1,0:T(8,128)(2,1)S(1)}, bf16[512,2048]{1,0:T(8,128)(2,1)}, u32[]{:S(2)}) copy-start(bf16[512,2048]{1,0:T(8,128)(2,1)} %copy-done.20) | copy-start | bytes 6291460
  174.1 5.2 %collective-permute-start.2 = (bf16[4,4,64,256]{3,2,1,0:T(8,128)(2,1)S(1)}, bf16[4,4,64,256]{3,2,1,0:T(8,128)(2,1)S(1)}, u32[]{:S(2)}, u32[]{:S(2)}) collective-permute-start(bf16[4,4,64,256]{3,2,1,0:T(8,128)(2,1)S(1)} %all-to-all-done.7), channel_id=1, source_target_pairs={{0,8},{8,0},{16,24},{24,16},{32,40},{40,32},{48,56},{56,48},{64,72... | collective-permute-start | bytes 1572872 | tf_op jit(solution)/shard_map/ppermute | solution.py:424
  179.5 1.5 copy-start.26
  179.5 4.9 %copy-start.29 = (s32[32,64]{1,0:T(8,128)S(1)}, s32[32,64]{1,0:T(8,128)}, u32[]{:S(2)}) copy-start(s32[32,64]{1,0:T(8,128)} %get-tuple-element.78) | copy-start | bytes 24580
  179.5 4.9 %copy-start.30 = (s32[1,2,4,4,64]{4,3,2,1,0:T(4,128)S(1)}, s32[1,2,4,4,64]{4,3,2,1,0:T(4,128)}, u32[]{:S(2)}) copy-start(s32[1,2,4,4,64]{4,3,2,1,0:T(4,128)} %get-tuple-element.79) | copy-start | bytes 24580
  179.5 5.0 %copy-start.25 = (bf16[8,256,256]{2,1,0:T(8,128)(2,1)S(1)}, bf16[8,256,256]{2,1,0:T(8,128)(2,1)}, u32[]{:S(2)}) copy-start(bf16[8,256,256]{2,1,0:T(8,128)(2,1)} %copy-done.24) | copy-start | bytes 3145732
  180.9 10.4 %all-to-all-start.8 = ((bf16[8,64,256]{2,1,0:T(8,128)(2,1)}), bf16[8,64,256]{2,1,0:T(8,128)(2,1)S(1)}, u32[]{:S(2)}, u32[]{:S(2)}) async-start(bf16[8,64,256]{2,1,0:T(8,128)(2,1)} %bitcast.15), calls=%async_computation.8 | async-start | bytes 524288 | tf_op jit(solution)/shard_map/all_to_all | solution.py:487
  192.2 16.4 %all-to-all-start.9 = ((f32[32,1,512]{2,1,0:T(1,128)}), f32[32,1,512]{2,1,0:T(1,128)S(1)}, u32[]{:S(2)}, u32[]{:S(2)}) async-start(f32[32,1,512]{2,1,0:T(1,128)} %reshape.100), calls=%async_computation.9 | async-start | bytes 131072 | tf_op jit(solution)/shard_map/all_to_all | solution.py:522
Sparse Core Ops, SparseCore 0:
  20.8 59.4 all-gather.2
  82.8 51.5 all-gather.4
Sparse Core Ops, SparseCore 1:
  124.5 60.3 reduce-scatter.1
